TPU v7x, 512 devices: a whole 4x8x8 slice. The times are simulated.
512 devices in a mesh: rows: 128 (over z, y, core), panel: 4 (over x).
Axes of the slice: x: 4, y: 8, z: 8, core: 2. Of those that a mesh axis runs over, the one named last changes fastest.
Arguments:
- columns: float32 [256, 524288], P('panel', 'rows'), as said below
- pivots: int32 [256], replicated, may hold values from 0 to 524287, as said below
- start: float32 [256, 32], replicated, may hold values from -6 to 6
Outputs:
- volumes: float32 [32, 524288], P(None, ('rows', 'panel'))
Inputs may be any that keep to these rules, and one draw needn't show every extreme that they name: `pivots`: distinct voxel indices; index 0 and 524287 are always among them; the voxel shards hold very unequal numbers of them. `columns`: real-valued entries.
All inputs are finite; a program needn't handle non-finite values.
Results may differ from a plain program's by a relative error of at most 0.003.
Values sent between devices are 32-bit elements; how exact they have to be, the bound alone decides.
No kernel may reach another device: no remote copies, remote signals or barrier semaphores. Data moves between devices by JAX's collectives and lax.ppermute only.
A program may use at most 64 MiB of HBM per device.

v0:
```python
import jax
import jax.numpy as jnp
from jax import lax
from jax.sharding import PartitionSpec as P

ITERS = 3


core_shift = 0.1


def lower_solve(factor, rhs):
    return lax.linalg.triangular_solve(factor, rhs, left_side=True, lower=True)


def upper_solve(factor, rhs):
    return lax.linalg.triangular_solve(factor, rhs, left_side=True, lower=True, transpose_a=True)


def pick_owned(local, pivots, offset):
    count = local.shape[1]
    where_local = pivots - offset
    owned = (where_local >= 0) & (where_local < count)
    taken = jnp.take(local, jnp.clip(where_local, 0, count - 1), axis=1)
    return jnp.where(owned[None, :], taken, jnp.zeros_like(taken))


def body(columns, pivots, start):
    highest = lax.Precision.HIGHEST
    width_dev = columns.shape[0]
    rows_dev = columns.shape[1]
    panels = lax.axis_size("panel")
    total_cols = width_dev * panels
    voxels = rows_dev * lax.axis_size("rows")
    row_index = lax.axis_index("rows")
    panel_index = lax.axis_index("panel")
    block = jnp.dot(
        columns,
        lax.all_gather(columns, "panel", axis=0, tiled=True).T,
        precision=highest,
        preferred_element_type=jnp.float32,
    )
    pivot_part = pick_owned(columns, pivots, row_index * rows_dev)
    block_sum, pivot_block = lax.psum((block, pivot_part), "rows")
    gram_sum, pivot_rows = (
        lax.all_gather(block_sum, "panel", axis=0, tiled=True),
        lax.all_gather(pivot_block, "panel", axis=0, tiled=True),
    )
    gram = gram_sum / voxels
    core = (
        jnp.dot(pivot_rows, pivot_rows.T, precision=highest, preferred_element_type=jnp.float32)
        / total_cols
    )
    core = core + core_shift * jnp.eye(total_cols, dtype=jnp.float32)
    core_factor = jnp.linalg.cholesky(core)
    basis = start
    for step in range(ITERS):
        pushed = jnp.dot(gram, basis, precision=highest, preferred_element_type=jnp.float32)
        image = upper_solve(core_factor, lower_solve(core_factor, pushed))
        small = jnp.dot(
            image.T,
            jnp.dot(gram, image, precision=highest, preferred_element_type=jnp.float32),
            precision=highest,
            preferred_element_type=jnp.float32,
        )
        small_factor = jnp.linalg.cholesky(small)
        basis = lower_solve(small_factor, image.T).T
    basis_part = lax.dynamic_slice_in_dim(basis, panel_index * width_dev, width_dev, 0)
    partial_volumes = jnp.dot(
        basis_part.T, columns, precision=highest, preferred_element_type=jnp.float32
    )
    return lax.psum_scatter(partial_volumes, "panel", scatter_dimension=1, tiled=True)


def solution(mesh):
    placed = (P("panel", "rows"), P(), P())
    return jax.shard_map(
        body, mesh=mesh, in_specs=placed, out_specs=P(None, ("rows", "panel")), check_vma=False
    )
```

profile of v0, /device:TPU:32, one launch (start us, length us, event | category | flops | bytes accessed | tf_op | source)
XLA Modules:
  0.0 407.8 jit_solution(6527301487536326858)
XLA Ops:
  6.5 0.7 all-gather.2.cloned.1.call-update
  7.3 1.8 copy.9
  9.2 0.7 gather_fusion
  9.9 0.8 select_bitcast_fusion
  10.7 56.7 %all-gather.2.cloned.1.call-done = f32[256,4096]{1,0:T(8,128)} async-done(((f32[64,4096]{1,0:T(8,128)}), f32[256,4096]{1,0:T(8,128)}) %all-gather.2.cloned.1.call-update) | async-done | bytes 4194320 | tf_op jit(solution)/shard_map/all_gather | solution.py:39
  67.4 6.8 %fusion.83 = f32[64,256]{1,0:T(8,128)} fusion(f32[64,4096]{1,0:T(8,128)S(1)} %copy-done.1, f32[256,4096]{1,0:T(8,128)} %all-gather.2.cloned.1.call-done), kind=kOutput, calls=%fused_computation.131 | convolution fusion | flops 805306368 | bytes 5308416 | tf_op jit(solution)/shard_map/dot_general | solution.py:37
  74.2 186.9 %all-reduce.4.cloned.1.call-done = (f32[64,256]{0,1:T(8,128)}, f32[64,256]{1,0:T(8,128)}) async-done(((f32[64,256]{0,1:T(8,128)}, f32[64,256]{1,0:T(8,128)}), (f32[64,256]{0,1:T(8,128)}, f32[64,256]{1,0:T(8,128)})) %all-reduce.4.cloned.1.call-update) | async-done | bytes 131088 | tf_op jit(solution)/shard_map/psum | solution.py:44
  261.1 1.0 copy.10
  262.1 12.7 %all_gather.9 = f32[256,256]{1,0:T(8,128)S(1)} all-gather(f32[64,256]{1,0:T(8,128)S(1)} %copy.10), channel_id=1, replica_groups=mesh['rows'=128,'panel'=4] {'panel'}, dimensions={0}, use_global_device_ids=true | all-gather | bytes 327680 | tf_op jit(solution)/shard_map/all_gather | solution.py:47
  275.2 12.7 %all_gather.11 = f32[256,256]{1,0:T(8,128)S(1)} all-gather(f32[64,256]{1,0:T(8,128)} %get-tuple-element.64), channel_id=1, replica_groups=mesh['rows'=128,'panel'=4] {'panel'}, dimensions={0}, use_global_device_ids=true | all-gather | bytes 327680 | tf_op jit(solution)/shard_map/all_gather | solution.py:46
  288.1 11.7 %cholesky.63 = f32[128,128]{1,0:T(8,128)S(1)} custom-call(f32[128,128]{1,0:T(8,128)S(1)} %cholesky.205), custom_call_target="Cholesky" | custom-call | tf_op jit(solution)/shard_map/jit(cholesky)/cholesky | solution.py:55
  299.8 9.8 %custom-call.22 = f32[1,128,128]{1,2,0:T(8,128)S(1)} custom-call(f32[1,128,128]{2,1,0:T(8,128)S(1)} %get-tuple-element.72), custom_call_target="InvertDiagBlocksLowerTriangular" | custom-call | tf_op jit(solution)/shard_map/jit(cholesky)/cholesky | solution.py:55
  310.2 11.7 %cholesky.130 = f32[128,128]{1,0:T(8,128)S(1)} custom-call(f32[128,128]{1,0:T(8,128)S(1)} %convolution_subtract_fusion), custom_call_target="Cholesky" | custom-call | tf_op jit(solution)/shard_map/jit(cholesky)/cholesky | solution.py:55
  321.9 0.7 compare_reduce_fusion.3
  324.1 4.3 %while.12 = (s32[]{:T(128)}, f32[256,256]{1,0:T(8,128)S(1)}, s32[2,2]{1,0:T(2,128)S(1)}, f32[2,128,128]{2,1,0:T(8,128)S(1)}, s32[]{:T(128)}) while((s32[]{:T(128)}, f32[256,256]{1,0:T(8,128)S(1)}, s32[2,2]{1,0:T(2,128)S(1)}, f32[2,128,128]{2,1,0:T(8,128)S(1)}, s32[]{:T(128)}) %tuple.46), condition=%wide.while_cond.1.clone.1, body=%wide.while_body.1.clone.1.sunk | while | flops 2 | bytes 131189 | solution.py:17
  324.9 1.4 bitcast_dynamic-update-slice_fusion.2
  326.9 1.4 bitcast_dynamic-update-slice_fusion.2
  328.4 19.7 %custom-call.36 = f32[2,128,128]{1,2,0:T(8,128)S(1)} custom-call(f32[2,128,128]{2,1,0:T(8,128)S(1)} %get-tuple-element.54), custom_call_target="InvertDiagBlocksLowerTriangular" | custom-call | tf_op jit(solution)/shard_map/triangular_solve/custom-call.5 | solution.py:17
  350.2 2.9 cholesky.174
  353.2 0.6 compare_reduce_fusion.2
  353.8 0.7 fusion.48
  354.5 2.4 custom-call.31
  359.4 2.9 cholesky.185
  362.3 0.6 compare_reduce_fusion.1
  363.0 0.7 fusion.49
  363.6 2.4 custom-call.34
  368.5 2.9 cholesky.196
  371.5 0.6 compare_reduce_fusion
  372.1 0.7 fusion.50
  372.8 2.4 custom-call.37
  375.5 1.4 fusion.64
  376.9 24.3 %reduce-scatter.2.cloned.1.call-done = f32[32,1024]{1,0:T(8,128)} async-done(((f32[32,4096]{1,0:T(8,128)}), f32[32,1024]{1,0:T(8,128)}) %reduce-scatter.2.cloned.1.call-update) | async-done | bytes 131088 | tf_op jit(solution)/shard_map/reduce_scatter | solution.py:72
  (69 shorter events, 9.7 us)
Async XLA Ops:
  6.5 341.5 %copy-start = (f32[256,32]{0,1:T(8,128)S(1)}, f32[256,32]{0,1:T(8,128)}, u32[]{:S(2)}) copy-start(f32[256,32]{0,1:T(8,128)} %param.12) | copy-start | bytes 98308
  6.5 60.8 %copy-start.1 = (f32[64,4096]{1,0:T(8,128)S(1)}, f32[64,4096]{1,0:T(8,128)}, u32[]{:S(2)}) copy-start(f32[64,4096]{1,0:T(8,128)} %param.10) | copy-start | bytes 3145732
  6.5 2.6 copy-start.2
  6.5 60.8 %all-gather.2.cloned.1.call-start = ((), (), s32[]{:S(2)}) async-start(), calls=%async_computation.1 | async-start | bytes 5242880 | tf_op jit(solution)/shard_map/all_gather | solution.py:39
  7.3 253.9 %all-reduce.4.cloned.1.call-start = ((), (), s32[]{:S(2)}) async-start(), calls=%async_computation.3 | async-start | bytes 393216 | tf_op jit(solution)/shard_map/psum | solution.py:44
  74.2 327.1 %reduce-scatter.2.cloned.1.call-start = ((), (), s32[]{:S(2)}) async-start(), calls=%async_computation.2 | async-start | bytes 655360 | tf_op jit(solution)/shard_map/reduce_scatter | solution.py:72
Sparse Core Ops, SparseCore 0:
  9.5 57.8 all-gather.1
  74.3 186.7 all-reduce.3
  377.1 24.1 reduce-scatter.1
where the time goes:
time: 408 us
  waiting for transfers between devices  269 us (66%)
  other arithmetic  74.7 us (18%)
  blocking collectives  25.3 us (6%)
  matrix products  15.9 us (4%)
  between operations  14.9 us (4%)
  local copies, waits for them, and re-layouts  8.04 us (2%)
    psum x1, waiting for transfers between devices, body(): block_sum, pivot_block = lax.psum((block, pivot_part), 'rows')  187 us
    all_gather x1, waiting for transfers between devices, body(): lax.all_gather(columns, 'panel', axis=0, tiled=True)  56.7 us
    another operation x6, other arithmetic, body(): core_factor = jnp.linalg.cholesky(core)  34 us
    reduce_scatter x1, waiting for transfers between devices, body(): lax.psum_scatter(partial_volumes, 'panel', scatter_dimension=1, tiled=True)  24.3 us
    another operation x4, other arithmetic, upper_solve(): lax.linalg.triangular_solve(factor, rhs, left_side=True, lower=True, tran...  19.7 us
    all_gather x1, blocking collectives, body(): lax.all_gather(pivot_block, 'panel', axis=0, tiled=True)  12.7 us
    all_gather x1, blocking collectives, body(): lax.all_gather(block_sum, 'panel', axis=0, tiled=True)  12.7 us
    another operation x9, other arithmetic, body(): small_factor = jnp.linalg.cholesky(small)  10.8 us
  transfers between devices with their start and end apart: 3, of which 3 were waited for; matrix products, arithmetic and copies ran while one was open for 1% of the time, Pallas kernels for 0%

commit v1 on v0

v1 whole, which is shorter than its diff:
```python
import jax
import jax.numpy as jnp
from jax import lax
from jax.sharding import Mesh, PartitionSpec as P

ITERS = 3
CORE_SHIFT = 0.1
HIGHEST = lax.Precision.HIGHEST

FAR = ("z", "y")
NEAR = ("core", "panel")


def dot(a, b):
    return jnp.dot(a, b, precision=HIGHEST, preferred_element_type=jnp.float32)


def lower_solve(factor, rhs):
    return lax.linalg.triangular_solve(factor, rhs, left_side=True, lower=True)


def upper_solve(factor, rhs):
    return lax.linalg.triangular_solve(factor, rhs, left_side=True, lower=True, transpose_a=True)


def sum_everywhere(part):
    rows, width = part.shape
    far = lax.axis_size(FAR)
    near = lax.axis_size(NEAR)
    pieces = lax.all_to_all(part.reshape(far, rows // far, width), FAR, 0, 0, tiled=True)
    piece = jnp.sum(pieces, axis=0)
    copies = jnp.broadcast_to(piece[None], (near, rows // far, width))
    piece = jnp.sum(lax.all_to_all(copies, NEAR, 0, 0, tiled=True), axis=0)
    copies = jnp.broadcast_to(piece[None], (far, rows // far, width))
    return lax.all_to_all(copies, FAR, 0, 0, tiled=True).reshape(rows, width)


def body(columns, pivots, start):
    total_cols = columns.shape[0] * lax.axis_size("panel")
    width = columns.shape[1] // lax.axis_size("panel")
    place = lax.axis_index(("z", "y", "core", "panel"))
    voxels = width * lax.axis_size(("z", "y", "core", "panel"))
    cols = lax.all_to_all(columns, "panel", 1, 0, tiled=True)
    here = jnp.arange(width, dtype=jnp.int32) + place * width
    chosen = jnp.any(pivots[:, None] == here[None, :], axis=0).astype(jnp.float32)
    gram_part = dot(cols, cols.T)
    core_part = dot(cols * chosen[None, :], cols.T)
    both = sum_everywhere(jnp.concatenate([gram_part, core_part], axis=0))
    gram = both[:total_cols] / voxels
    core = both[total_cols:] / total_cols + CORE_SHIFT * jnp.eye(total_cols, dtype=jnp.float32)
    core_factor = jnp.linalg.cholesky(core)
    basis = start
    for step in range(ITERS):
        pushed = dot(gram, basis)
        image = upper_solve(core_factor, lower_solve(core_factor, pushed))
        small = dot(image.T, dot(gram, image))
        small_factor = jnp.linalg.cholesky(small)
        basis = lower_solve(small_factor, image.T).T
    return dot(basis.T, cols)


def solution(mesh):
    fine = Mesh(mesh.devices.reshape(8, 8, 2, 4), ("z", "y", "core", "panel"))
    rows = ("z", "y", "core")
    return jax.shard_map(
        body,
        mesh=fine,
        in_specs=(P("panel", rows), P(), P()),
        out_specs=P(None, rows + ("panel",)),
        check_vma=False,
    )
```

time: 408 us -> 182 us (0.45)
  the two profiles are of different devices: /device:TPU:32 before, /device:TPU:8 now
where the time goes in v1:
time: 182 us
  other arithmetic  74.6 us (41%)
  blocking collectives  42.4 us (23%)
  waiting for transfers between devices  33.7 us (19%)
  matrix products  10.6 us (6%)
  starting transfers between devices  9.6 us (5%)
  local copies, waits for them, and re-layouts  8.93 us (5%)
    all_to_all x1, blocking collectives, sum_everywhere(): lax.all_to_all(part.reshape(far, rows // far, width), FAR, 0, 0, tiled=True)  34.6 us
    another operation x6, other arithmetic, body(): core_factor = jnp.linalg.cholesky(core)  34 us
    another operation x4, other arithmetic, upper_solve(): lax.linalg.triangular_solve(factor, rhs, left_side=True, lower=True, tran...  19.9 us
    all_to_all x1, waiting for transfers between devices, sum_everywhere(): return lax.all_to_all(copies, FAR, 0, 0, tiled=True).reshape(rows, width)  19.5 us
    all_to_all x1, waiting for transfers between devices, body(): cols = lax.all_to_all(columns, 'panel', 1, 0, tiled=True)  14.2 us
    another operation x9, other arithmetic, body(): small_factor = jnp.linalg.cholesky(small)  10.8 us
    another operation x6, other arithmetic, lower_solve(): return lax.linalg.triangular_solve(factor, rhs, left_side=True, lower=True)  9.26 us
    all_to_all x1, blocking collectives, sum_everywhere(): piece = jnp.sum(lax.all_to_all(copies, NEAR, 0, 0, tiled=True), axis=0)  7.73 us
  transfers between devices with their start and end apart: 2, of which 2 were waited for; matrix products, arithmetic and copies ran while one was open for 0% of the time, Pallas kernels for 0%

profile of v1, /device:TPU:8, one launch (start us, length us, event | category | flops | bytes accessed | tf_op | source)
XLA Modules:
  0.0 181.6 jit_solution(14411463496410476037)
XLA Ops:
  0.0 2.3 %copy.80 = f32[8,4,8,1024]{3,2,0,1:T(8,128)} copy(f32[8,4,8,1024]{3,2,1,0:T(8,128)} %bitcast.150) | data formatting | bytes 2097152 | tf_op jit(solution)/shard_map/all_to_all | solution.py:43
  2.3 4.3 %all-to-all-start = ((f32[64,4,1024]{2,0,1:T(8,128)}), f32[64,4,1024]{2,0,1:T(8,128)S(1)}, u32[]{:S(2)}, u32[]{:S(2)}) async-start(f32[64,4,1024]{2,0,1:T(8,128)} %bitcast.139), calls=%async_computation | async-start | bytes 2097152 | tf_op jit(solution)/shard_map/all_to_all | solution.py:43
  6.6 0.7 copy-done.1
  7.5 14.2 %all-to-all-done = f32[64,4,1024]{2,0,1:T(8,128)S(1)} async-done(((f32[64,4,1024]{2,0,1:T(8,128)}), f32[64,4,1024]{2,0,1:T(8,128)S(1)}, u32[]{:S(2)}, u32[]{:S(2)}) %all-to-all-start) | async-done | bytes 1048608 | tf_op jit(solution)/shard_map/all_to_all | solution.py:43
  21.7 1.0 fusion.77
  22.9 1.0 fusion.78
  24.0 34.6 %all_to_all.34 = f32[64,8,256]{2,1,0:T(8,128)S(1)} all-to-all(f32[64,8,256]{2,1,0:T(8,128)S(1)} %maximum_bitcast_fusion), channel_id=1, replica_groups=mesh['z'=8,'y'=8,'core'=2,'panel'=4] {'z','y'}, dimensions={0} | all-to-all | bytes 1048576 | tf_op jit(solution)/shard_map/all_to_all | solution.py:30
  58.7 7.7 %all_to_all.35 = f32[8,8,256]{2,1,0:T(8,128)S(1)} all-to-all(f32[8,8,256]{2,1,0:T(8,128)S(1)} %broadcast_in_dim.5), channel_id=1, replica_groups=mesh['z'=8,'y'=8,'core'=2,'panel'=4] {'core','panel'}, dimensions={0} | all-to-all | bytes 131072 | tf_op jit(solution)/shard_map/all_to_all | solution.py:33
  66.4 0.8 broadcast_in_dim.6
  67.3 5.3 %all-to-all-start.3 = ((f32[64,8,256]{2,1,0:T(8,128)}), f32[64,8,256]{2,1,0:T(8,128)S(1)}, u32[]{:S(2)}, u32[]{:S(2)}) async-start(f32[64,8,256]{2,1,0:T(8,128)} %broadcast_in_dim.6), calls=%async_computation.3 | async-start | bytes 1048576 | tf_op jit(solution)/shard_map/all_to_all | solution.py:35
  72.6 19.5 %all-to-all-done.3 = f32[64,8,256]{2,1,0:T(8,128)S(1)} async-done(((f32[64,8,256]{2,1,0:T(8,128)}), f32[64,8,256]{2,1,0:T(8,128)S(1)}, u32[]{:S(2)}, u32[]{:S(2)}) %all-to-all-start.3) | async-done | bytes 524320 | tf_op jit(solution)/shard_map/all_to_all | solution.py:35
  92.5 11.7 %cholesky.63 = f32[128,128]{1,0:T(8,128)S(1)} custom-call(f32[128,128]{1,0:T(8,128)S(1)} %cholesky.205), custom_call_target="Cholesky" | custom-call | tf_op jit(solution)/shard_map/jit(cholesky)/cholesky | solution.py:51
  104.2 9.8 %custom-call.22 = f32[1,128,128]{1,2,0:T(8,128)S(1)} custom-call(f32[1,128,128]{2,1,0:T(8,128)S(1)} %get-tuple-element.186), custom_call_target="InvertDiagBlocksLowerTriangular" | custom-call | tf_op jit(solution)/shard_map/jit(cholesky)/cholesky | solution.py:51
  114.5 11.7 %cholesky.130 = f32[128,128]{1,0:T(8,128)S(1)} custom-call(f32[128,128]{1,0:T(8,128)S(1)} %convolution_subtract_fusion), custom_call_target="Cholesky" | custom-call | tf_op jit(solution)/shard_map/jit(cholesky)/cholesky | solution.py:51
  126.6 0.7 compare_reduce_fusion.4
  128.7 4.3 %while.12 = (s32[]{:T(128)}, f32[256,256]{0,1:T(8,128)S(1)}, s32[2,2]{1,0:T(2,128)S(1)}, f32[2,128,128]{2,1,0:T(8,128)S(1)}, s32[]{:T(128)}) while((s32[]{:T(128)}, f32[256,256]{0,1:T(8,128)S(1)}, s32[2,2]{1,0:T(2,128)S(1)}, f32[2,128,128]{2,1,0:T(8,128)S(1)}, s32[]{:T(128)}) %tuple.72), condition=%wide.while_cond.1.clone.1, body=%wide.while_body.1.clone.1.sunk | while | flops 2 | bytes 393321 | solution.py:23
  128.7 0.7 fusion.110
  129.4 1.3 dynamic-slice.18
  130.9 0.7 fusion.110
  131.5 1.3 dynamic-slice.18
  133.0 19.9 %custom-call.36 = f32[2,128,128]{1,2,0:T(8,128)S(1)} custom-call(f32[2,128,128]{2,1,0:T(8,128)S(1)} %get-tuple-element.54), custom_call_target="InvertDiagBlocksLowerTriangular" | custom-call | tf_op jit(solution)/shard_map/triangular_solve/custom-call.5 | solution.py:23
  155.1 2.9 %cholesky.174 = f32[32,32]{1,0:T(8,128)S(1)} custom-call(f32[32,32]{1,0:T(8,128)S(1)} %fusion.56), custom_call_target="Cholesky" | custom-call | tf_op jit(solution)/shard_map/jit(cholesky)/cholesky | solution.py:57
  158.7 0.7 fusion.45
  159.3 2.4 %custom-call.31 = f32[1,32,32]{1,2,0:T(8,128)S(1)} custom-call(f32[1,32,32]{2,1,0:T(8,128)S(1)} %fusion.45), custom_call_target="InvertDiagBlocksLowerTriangular" | custom-call | tf_op jit(solution)/shard_map/triangular_solve/custom-call.6 | solution.py:19
  164.2 2.9 %cholesky.185 = f32[32,32]{1,0:T(8,128)S(1)} custom-call(f32[32,32]{1,0:T(8,128)S(1)} %fusion.54), custom_call_target="Cholesky" | custom-call | tf_op jit(solution)/shard_map/jit(cholesky)/cholesky | solution.py:57
  167.8 0.7 fusion.46
  168.4 2.4 %custom-call.34 = f32[1,32,32]{1,2,0:T(8,128)S(1)} custom-call(f32[1,32,32]{2,1,0:T(8,128)S(1)} %fusion.46), custom_call_target="InvertDiagBlocksLowerTriangular" | custom-call | tf_op jit(solution)/shard_map/triangular_solve/custom-call.6 | solution.py:19
  173.3 2.9 %cholesky.196 = f32[32,32]{1,0:T(8,128)S(1)} custom-call(f32[32,32]{1,0:T(8,128)S(1)} %fusion.52), custom_call_target="Cholesky" | custom-call | tf_op jit(solution)/shard_map/jit(cholesky)/cholesky | solution.py:57
  176.2 0.6 compare_reduce_fusion.1
  176.9 0.7 fusion.47
  177.5 2.4 %custom-call.37 = f32[1,32,32]{1,2,0:T(8,128)S(1)} custom-call(f32[1,32,32]{2,1,0:T(8,128)S(1)} %fusion.47), custom_call_target="InvertDiagBlocksLowerTriangular" | custom-call | tf_op jit(solution)/shard_map/triangular_solve/custom-call.6 | solution.py:19
  180.2 1.4 fusion.79
  (78 shorter events, 10.3 us)
Async XLA Ops:
  0.0 152.9 %copy-start = (f32[256,32]{0,1:T(8,128)S(1)}, f32[256,32]{0,1:T(8,128)}, u32[]{:S(2)}) copy-start(f32[256,32]{0,1:T(8,128)} %param.12) | copy-start | bytes 98308
  2.3 19.4 %all-to-all-start = ((f32[64,4,1024]{2,0,1:T(8,128)}), f32[64,4,1024]{2,0,1:T(8,128)S(1)}, u32[]{:S(2)}, u32[]{:S(2)}) async-start(f32[64,4,1024]{2,0,1:T(8,128)} %bitcast.139), calls=%async_computation | async-start | bytes 2097152 | tf_op jit(solution)/shard_map/all_to_all | solution.py:43
  6.6 0.7 copy-start.1
  67.3 24.8 %all-to-all-start.3 = ((f32[64,8,256]{2,1,0:T(8,128)}), f32[64,8,256]{2,1,0:T(8,128)S(1)}, u32[]{:S(2)}, u32[]{:S(2)}) async-start(f32[64,8,256]{2,1,0:T(8,128)} %broadcast_in_dim.6), calls=%async_computation.3 | async-start | bytes 1048576 | tf_op jit(solution)/shard_map/all_to_all | solution.py:35

commit v2 on v1

v2 whole, which is shorter than its diff:
```python
import functools

import jax
import jax.numpy as jnp
from jax import lax
from jax.experimental import pallas as pl
from jax.experimental.pallas import tpu as pltpu
from jax.sharding import Mesh, PartitionSpec as P

ITERS = 3
CORE_SHIFT = 0.1
HIGHEST = lax.Precision.HIGHEST
SUB = 8
LANES = 128
BLOCK = 32

FAR = ("z", "y")
NEAR = ("core", "panel")
ROWS = ("z", "y", "core")


def dot(a, b, dims=(((1,), (0,)), ((), ()))):
    return lax.dot_general(a, b, dims, precision=HIGHEST, preferred_element_type=jnp.float32)


def inverse_factor(square, size):
    blocks = size // SUB
    row = lax.broadcasted_iota(jnp.int32, (SUB, LANES), 0)
    lane = lax.broadcasted_iota(jnp.int32, (SUB, LANES), 1)
    def spread(tile, r):
        return jnp.broadcast_to(tile[r : r + 1, :], (SUB, LANES))
    cols = [[None] * blocks for _ in range(size)]
    for j in range(size):
        for q in range(j // SUB, blocks):
            cols[j][q] = jnp.broadcast_to(square[SUB * q : SUB * q + SUB, j : j + 1], (SUB, LANES))
    inv = [[None] * blocks for _ in range(size)]
    roots = [jnp.zeros((SUB, LANES), jnp.float32) for _ in range(blocks)]
    for k in range(size):
        kq, kr = divmod(k, SUB)
        pivot = spread(cols[k][kq], kr)
        recip = 1.0 / pivot
        roots[kq] = jnp.where(row == kr, lax.rsqrt(pivot), roots[kq])
        lower = list(cols[k])
        lower[kq] = jnp.where(row > kr, cols[k][kq], 0.0)
        lower = [None if t is None else t * recip for t in lower]
        for j in range(k + 1, size):
            jq, jr = divmod(j, SUB)
            factor = spread(cols[k][jq], jr)
            for q in range(jq, blocks):
                cols[j][q] = cols[j][q] - lower[q] * factor
        inv[k][kq] = jnp.where(row == kr, 1.0, 0.0) - lower[kq]
        for q in range(kq + 1, blocks):
            inv[k][q] = -lower[q]
        for j in range(k):
            factor = spread(inv[j][kq], kr)
            for q in range(kq, blocks):
                inv[j][q] = inv[j][q] - lower[q] * factor
    out = []
    for q in range(blocks):
        tile = jnp.zeros((SUB, LANES), jnp.float32)
        for j in range(min(size, SUB * (q + 1))):
            tile = jnp.where(lane == j, inv[j][q], tile)
        out.append(tile * roots[q])
    return jnp.concatenate(out, axis=0)[:, :size]


def solve_kernel(voxels, both_ref, start_ref, cols_ref, out_ref, gram, work):
    size = cols_ref.shape[0]
    rank = start_ref.shape[1]
    every_row = lax.broadcasted_iota(jnp.int32, (size, size), 0)
    every_lane = lax.broadcasted_iota(jnp.int32, (size, size), 1)
    gram[...] = both_ref[:size, :] * (1.0 / voxels)
    work[...] = both_ref[size:, :] * (1.0 / size) + jnp.where(every_row == every_lane, CORE_SHIFT, 0.0)

    lane = lax.broadcasted_iota(jnp.int32, (BLOCK, size), 1)
    row = lax.broadcasted_iota(jnp.int32, (BLOCK, size), 0)

    def sweep(step, carry):
        base = step * BLOCK
        band = work[pl.ds(pl.multiple_of(base, BLOCK), BLOCK), :]
        factor = inverse_factor(pltpu.roll(band, size - base, axis=1)[:, :LANES], BLOCK)
        inside = (lane >= base) & (lane < base + BLOCK)
        band = jnp.where(inside, jnp.where(lane - base == row, -1.0, 0.0), band)
        scaled = dot(factor, band)
        outer = dot(scaled, scaled, (((0,), (0,)), ((), ())))
        keep_row = (every_row < base) | (every_row >= base + BLOCK)
        keep_lane = (every_lane < base) | (every_lane >= base + BLOCK)
        work[...] = jnp.where(keep_row & keep_lane, work[...], 0.0) - outer
        return carry

    lax.fori_loop(0, size // BLOCK, sweep, 0)

    def iterate(step, carry):
        image, _ = carry
        pushed = dot(gram[...], image)
        small = dot(image, pushed, (((0,), (0,)), ((), ())))
        small = jnp.concatenate([small, jnp.zeros((rank, LANES - rank), jnp.float32)], axis=1)
        factor = inverse_factor(small, rank)
        basis = dot(image, factor, (((1,), (1,)), ((), ())))
        return -dot(work[...], dot(pushed, factor, (((1,), (1,)), ((), ())))), basis

    image = -dot(work[...], dot(gram[...], start_ref[...]))
    _, basis = lax.fori_loop(0, ITERS, iterate, (image, image))
    out_ref[...] = dot(basis, cols_ref[...], (((0,), (0,)), ((), ())))


def solve(both, start, cols, voxels):
    size, width = cols.shape
    return pl.pallas_call(
        functools.partial(solve_kernel, voxels),
        out_shape=jax.ShapeDtypeStruct((start.shape[1], width), jnp.float32),
        in_specs=[pl.BlockSpec(memory_space=pltpu.VMEM)] * 3,
        out_specs=pl.BlockSpec(memory_space=pltpu.VMEM),
        scratch_shapes=[pltpu.VMEM((size, size), jnp.float32)] * 2,
        compiler_params=pltpu.CompilerParams(vmem_limit_bytes=32 * 2**20),
        name="solve",
    )(both, start, cols)


def sum_everywhere(part):
    rows, width = part.shape
    far = lax.axis_size(FAR)
    near = lax.axis_size(NEAR)
    pieces = lax.all_to_all(part.reshape(far, rows // far, width), FAR, 0, 0, tiled=True)
    piece = jnp.sum(pieces, axis=0)
    copies = jnp.broadcast_to(piece[None], (near, rows // far, width))
    piece = jnp.sum(lax.all_to_all(copies, NEAR, 0, 0, tiled=True), axis=0)
    copies = jnp.broadcast_to(piece[None], (far, rows // far, width))
    return lax.all_to_all(copies, FAR, 0, 0, tiled=True).reshape(rows, width)


def body(columns, pivots, start):
    width = columns.shape[1] // lax.axis_size("panel")
    place = lax.axis_index(ROWS + ("panel",))
    voxels = width * lax.axis_size(ROWS + ("panel",))
    cols = lax.all_to_all(columns, "panel", 1, 0, tiled=True)
    here = jnp.arange(width, dtype=jnp.int32) + place * width
    chosen = jnp.any(pivots[:, None] == here[None, :], axis=0).astype(jnp.float32)
    gram_part = dot(cols, cols.T)
    core_part = dot(cols * chosen[None, :], cols.T)
    both = sum_everywhere(jnp.concatenate([gram_part, core_part], axis=0))
    return solve(both, start, cols, voxels)


def solution(mesh):
    fine = Mesh(mesh.devices.reshape(8, 8, 2, 4), ROWS + ("panel",))
    return jax.shard_map(
        body,
        mesh=fine,
        in_specs=(P("panel", ROWS), P(), P()),
        out_specs=P(None, ROWS + ("panel",)),
        check_vma=False,
    )
```

time: 182 us -> 115 us (0.63)
  other arithmetic: 74.6 us -> 0.45 us
  Pallas kernels: 0 us -> 22.8 us
  matrix products: 10.6 us -> 2.07 us
  local copies, waits for them, and re-layouts: 8.93 us -> 3.93 us
    another operation x25 -> x0, other arithmetic: 74 us -> none  [the longest x6 34 us: body(): core_factor = jnp.linalg.cholesky(core)]
    pallas_call x0 -> x1, Pallas kernels: none -> 22.8 us  [solve(): pl.pallas_call(functools.partial(solve_kernel, voxels), out_shape=jax.Sha...]
    another operation x18 -> x0, local copies, waits for them, and re-layouts: 4.61 us -> none  [the longest x11 4.29 us: upper_solve(): lax.linalg.triangular_solve(factor, rhs, left_side=True, lower=True, tran...]
    another operation x23 -> x0, matrix products: 4.54 us -> none  [the longest x12 2.21 us: lower_solve(): return lax.linalg.triangular_solve(factor, rhs, left_side=True, lower=True)]
    dot_general x12 -> x2, matrix products: 6.04 us -> 2.07 us  [dot(): lax.dot_general(a, b, dims, precision=HIGHEST, preferred_element_type=jnp...]
where the time goes in v2:
time: 115 us
  blocking collectives  42.4 us (37%)
  waiting for transfers between devices  33.6 us (29%)
  Pallas kernels  22.8 us (20%)
  starting transfers between devices  9.72 us (8%)
  local copies, waits for them, and re-layouts  3.93 us (3%)
  matrix products  2.07 us (2%)
    all_to_all x1, blocking collectives, sum_everywhere(): lax.all_to_all(part.reshape(far, rows // far, width), FAR, 0, 0, tiled=True)  34.6 us
    pallas_call x1, Pallas kernels, solve(): pl.pallas_call(functools.partial(solve_kernel, voxels), out_shape=jax.Sha...  22.8 us
    all_to_all x1, waiting for transfers between devices, sum_everywhere(): return lax.all_to_all(copies, FAR, 0, 0, tiled=True).reshape(rows, width)  19.4 us
    all_to_all x1, waiting for transfers between devices, body(): cols = lax.all_to_all(columns, 'panel', 1, 0, tiled=True)  14.2 us
    all_to_all x1, blocking collectives, sum_everywhere(): piece = jnp.sum(lax.all_to_all(copies, NEAR, 0, 0, tiled=True), axis=0)  7.73 us
    all_to_all x1, starting transfers between devices, sum_everywhere(): return lax.all_to_all(copies, FAR, 0, 0, tiled=True).reshape(rows, width)  5.43 us
    all_to_all x1, starting transfers between devices, body(): cols = lax.all_to_all(columns, 'panel', 1, 0, tiled=True)  4.29 us
    all_to_all x1, local copies, waits for them, and re-layouts, body(): cols = lax.all_to_all(columns, 'panel', 1, 0, tiled=True)  2.33 us
  transfers between devices with their start and end apart: 2, of which 2 were waited for; matrix products, arithmetic and copies ran while one was open for 0% of the time, Pallas kernels for 0%

profile of v2, /device:TPU:8, one launch (start us, length us, event | category | flops | bytes accessed | tf_op | source)
XLA Modules:
  0.0 115.0 jit_solution(12421791823595119335)
XLA Ops:
  0.0 2.3 %copy.10 = f32[8,4,8,1024]{3,2,0,1:T(8,128)} copy(f32[8,4,8,1024]{3,2,1,0:T(8,128)} %bitcast.21) | data formatting | bytes 2097152 | tf_op jit(solution)/shard_map/all_to_all | solution.py:136
  2.3 4.3 %all-to-all-start = ((f32[64,4,1024]{2,0,1:T(8,128)}), f32[64,4,1024]{2,0,1:T(8,128)S(1)}, u32[]{:S(2)}, u32[]{:S(2)}) async-start(f32[64,4,1024]{2,0,1:T(8,128)} %bitcast.15), calls=%async_computation | async-start | bytes 2097152 | tf_op jit(solution)/shard_map/all_to_all | solution.py:136
  6.6 0.0 copy-start.1
  6.6 0.7 copy-done.1
  7.3 0.2 compare_reduce_fusion
  7.5 14.2 %all-to-all-done = f32[64,4,1024]{2,0,1:T(8,128)S(1)} async-done(((f32[64,4,1024]{2,0,1:T(8,128)}), f32[64,4,1024]{2,0,1:T(8,128)S(1)}, u32[]{:S(2)}, u32[]{:S(2)}) %all-to-all-start) | async-done | bytes 1048608 | tf_op jit(solution)/shard_map/all_to_all | solution.py:136
  21.7 1.0 fusion
  22.8 0.1 bitcast_multiply_fusion
  22.9 1.0 fusion.1
  24.0 34.6 %all_to_all.34 = f32[64,8,256]{2,1,0:T(8,128)S(1)} all-to-all(f32[64,8,256]{2,1,0:T(8,128)S(1)} %maximum_bitcast_fusion), channel_id=1, replica_groups=mesh['z'=8,'y'=8,'core'=2,'panel'=4] {'z','y'}, dimensions={0} | all-to-all | bytes 1048576 | tf_op jit(solution)/shard_map/all_to_all | solution.py:124
  58.6 0.1 reduce_sum.18
  58.7 7.7 %all_to_all.35 = f32[8,8,256]{2,1,0:T(8,128)S(1)} all-to-all(f32[8,8,256]{2,1,0:T(8,128)S(1)} %broadcast_in_dim.4), channel_id=1, replica_groups=mesh['z'=8,'y'=8,'core'=2,'panel'=4] {'core','panel'}, dimensions={0} | all-to-all | bytes 131072 | tf_op jit(solution)/shard_map/all_to_all | solution.py:127
  66.4 0.8 broadcast_in_dim.5
  67.3 0.0 copy-start
  67.3 5.4 %all-to-all-start.3 = ((f32[64,8,256]{2,1,0:T(8,128)}), f32[64,8,256]{2,1,0:T(8,128)S(1)}, u32[]{:S(2)}, u32[]{:S(2)}) async-start(f32[64,8,256]{2,1,0:T(8,128)} %broadcast_in_dim.5), calls=%async_computation.3 | async-start | bytes 1048576 | tf_op jit(solution)/shard_map/all_to_all | solution.py:129
  72.7 0.0 copy-done
  72.7 0.1 copy.7.start_ref
  72.8 19.4 %all-to-all-done.3 = f32[64,8,256]{2,1,0:T(8,128)S(1)} async-done(((f32[64,8,256]{2,1,0:T(8,128)}), f32[64,8,256]{2,1,0:T(8,128)S(1)}, u32[]{:S(2)}, u32[]{:S(2)}) %all-to-all-start.3) | async-done | bytes 524320 | tf_op jit(solution)/shard_map/all_to_all | solution.py:129
  92.2 22.8 %solve.1 = f32[32,1024]{1,0:T(8,128)} custom-call(f32[512,256]{1,0:T(8,128)S(1)} %bitcast.19, f32[256,32]{1,0:T(8,128)S(1)} %copy.7.start_ref, f32[256,1024]{1,0:T(8,128)S(1)} %bitcast.18), custom_call_target="tpu_custom_call" | custom-call | tf_op jit(solution)/shard_map/solve/pallas_call | solution.py:109
  (5 shorter events, 0.1 us)
Async XLA Ops:
  2.3 19.4 %all-to-all-start = ((f32[64,4,1024]{2,0,1:T(8,128)}), f32[64,4,1024]{2,0,1:T(8,128)S(1)}, u32[]{:S(2)}, u32[]{:S(2)}) async-start(f32[64,4,1024]{2,0,1:T(8,128)} %bitcast.15), calls=%async_computation | async-start | bytes 2097152 | tf_op jit(solution)/shard_map/all_to_all | solution.py:136
  6.6 0.7 copy-start.1
  67.3 5.4 %copy-start = (f32[256,32]{0,1:T(8,128)S(1)}, f32[256,32]{0,1:T(8,128)}, u32[]{:S(2)}) copy-start(f32[256,32]{0,1:T(8,128)} %param.5) | copy-start | bytes 98308
  67.3 24.9 %all-to-all-start.3 = ((f32[64,8,256]{2,1,0:T(8,128)}), f32[64,8,256]{2,1,0:T(8,128)S(1)}, u32[]{:S(2)}, u32[]{:S(2)}) async-start(f32[64,8,256]{2,1,0:T(8,128)} %broadcast_in_dim.5), calls=%async_computation.3 | async-start | bytes 1048576 | tf_op jit(solution)/shard_map/all_to_all | solution.py:129

commit v3 on v2

--- a/solution.py
+++ b/solution.py
@@ -13,6 +13,7 @@
 SUB = 8
 LANES = 128
 BLOCK = 32
+SUBS = 2
 
 FAR = ("z", "y")
 NEAR = ("core", "panel")
@@ -64,13 +65,62 @@
     return jnp.concatenate(out, axis=0)[:, :size]
 
 
-def solve_kernel(voxels, both_ref, start_ref, cols_ref, out_ref, gram, work):
+def pack_kernel(cols_ref, chosen_ref, out_ref):
+    far, subs, width = out_ref.shape
+    size = cols_ref.shape[0]
+    each = size // far // subs
+    cols = cols_ref[...]
+    picked = cols * chosen_ref[...]
+    both_lanes = (((1,), (1,)), ((), ()))
+    gram = dot(cols, cols, both_lanes)
+    core = dot(picked, cols, both_lanes)
+    row = lax.broadcasted_iota(jnp.int32, (size, size), 0)
+    lane = lax.broadcasted_iota(jnp.int32, (size, size), 1)
+    packed = jnp.where(row >= lane, gram, core)
+    diagonal = jnp.sum(jnp.where(row == lane, core, 0.0), axis=1, keepdims=True)
+    spare = width - each * size
+    spare_lane = lax.broadcasted_iota(jnp.int32, (far, spare), 1)
+    for r in range(subs):
+        tail = jnp.zeros((far, spare), jnp.float32)
+        for h in range(each):
+            first = (r * each + h) * far
+            out_ref[:, r, h * size : (h + 1) * size] = packed[first : first + far, :]
+            tail = jnp.where(spare_lane == h, diagonal[first : first + far, :], tail)
+        out_ref[:, r, each * size :] = tail
+
+
+def pack(cols, chosen, far):
+    size = cols.shape[0]
+    each = size // far // SUBS
+    return pl.pallas_call(
+        pack_kernel,
+        out_shape=jax.ShapeDtypeStruct((far, SUBS, each * size + LANES), jnp.float32),
+        in_specs=[pl.BlockSpec(memory_space=pltpu.VMEM)] * 2,
+        out_specs=pl.BlockSpec(memory_space=pltpu.VMEM),
+        compiler_params=pltpu.CompilerParams(vmem_limit_bytes=32 * 2**20),
+        name="pack",
+    )(cols, chosen)
+
+
+def solve_kernel(voxels, packed_ref, start_ref, cols_ref, out_ref, gram, work):
     size = cols_ref.shape[0]
     rank = start_ref.shape[1]
+    far, subs, width = packed_ref.shape
+    each = size // far // subs
     every_row = lax.broadcasted_iota(jnp.int32, (size, size), 0)
     every_lane = lax.broadcasted_iota(jnp.int32, (size, size), 1)
-    gram[...] = both_ref[:size, :] * (1.0 / voxels)
-    work[...] = both_ref[size:, :] * (1.0 / size) + jnp.where(every_row == every_lane, CORE_SHIFT, 0.0)
+    rows, diagonal = [], []
+    for r in range(subs):
+        tail = packed_ref[:, r, each * size :]
+        for h in range(each):
+            rows.append(packed_ref[:, r, h * size : (h + 1) * size])
+            diagonal.append(tail[:, h : h + 1])
+    packed = jnp.concatenate(rows, axis=0)
+    flipped = packed.T
+    gram[...] = jnp.where(every_row >= every_lane, packed, flipped) * (1.0 / voxels)
+    core = jnp.where(every_row < every_lane, packed, flipped)
+    core = jnp.where(every_row == every_lane, jnp.concatenate(diagonal, axis=0), core) * (1.0 / size)
+    work[...] = core + jnp.where(every_row == every_lane, CORE_SHIFT, 0.0)
 
     lane = lax.broadcasted_iota(jnp.int32, (BLOCK, size), 1)
     row = lax.broadcasted_iota(jnp.int32, (BLOCK, size), 0)
@@ -104,7 +154,7 @@
     out_ref[...] = dot(basis, cols_ref[...], (((0,), (0,)), ((), ())))
 
 
-def solve(both, start, cols, voxels):
+def solve(packed, start, cols, voxels):
     size, width = cols.shape
     return pl.pallas_call(
         functools.partial(solve_kernel, voxels),
@@ -114,19 +164,17 @@
         scratch_shapes=[pltpu.VMEM((size, size), jnp.float32)] * 2,
         compiler_params=pltpu.CompilerParams(vmem_limit_bytes=32 * 2**20),
         name="solve",
-    )(both, start, cols)
+    )(packed, start, cols)
 
 
-def sum_everywhere(part):
-    rows, width = part.shape
-    far = lax.axis_size(FAR)
+def sum_everywhere(pieces):
+    far, subs, width = pieces.shape
     near = lax.axis_size(NEAR)
-    pieces = lax.all_to_all(part.reshape(far, rows // far, width), FAR, 0, 0, tiled=True)
-    piece = jnp.sum(pieces, axis=0)
-    copies = jnp.broadcast_to(piece[None], (near, rows // far, width))
+    piece = jnp.sum(lax.all_to_all(pieces, FAR, 0, 0, tiled=True), axis=0)
+    copies = jnp.broadcast_to(piece[None], (near, subs, width))
     piece = jnp.sum(lax.all_to_all(copies, NEAR, 0, 0, tiled=True), axis=0)
-    copies = jnp.broadcast_to(piece[None], (far, rows // far, width))
-    return lax.all_to_all(copies, FAR, 0, 0, tiled=True).reshape(rows, width)
+    copies = jnp.broadcast_to(piece[None], (far, subs, width))
+    return lax.all_to_all(copies, FAR, 0, 0, tiled=True)
 
 
 def body(columns, pivots, start):
@@ -135,11 +183,9 @@
     voxels = width * lax.axis_size(ROWS + ("panel",))
     cols = lax.all_to_all(columns, "panel", 1, 0, tiled=True)
     here = jnp.arange(width, dtype=jnp.int32) + place * width
-    chosen = jnp.any(pivots[:, None] == here[None, :], axis=0).astype(jnp.float32)
-    gram_part = dot(cols, cols.T)
-    core_part = dot(cols * chosen[None, :], cols.T)
-    both = sum_everywhere(jnp.concatenate([gram_part, core_part], axis=0))
-    return solve(both, start, cols, voxels)
+    chosen = jnp.any(pivots[:, None] == here[None, :], axis=0, keepdims=True).astype(jnp.float32)
+    packed = sum_everywhere(pack(cols, chosen, lax.axis_size(FAR)))
+    return solve(packed, start, cols, voxels)
 
 
 def solution(mesh):

time: 115 us -> 108 us (0.939)
  blocking collectives: 42.4 us -> 38.5 us
  waiting for transfers between devices: 33.6 us -> 30.2 us
  Pallas kernels: 22.8 us -> 25 us
  matrix products: 2.07 us -> 0 us
    all_to_all x1, blocking collectives: 34.6 us -> 30.8 us  [sum_everywhere(): piece = jnp.sum(lax.all_to_all(pieces, FAR, 0, 0, tiled=True), axis=0)]
    all_to_all x1, waiting for transfers between devices: 19.4 us -> 16 us  [sum_everywhere(): return lax.all_to_all(copies, FAR, 0, 0, tiled=True)]
    dot_general x2 -> x0, matrix products: 2.07 us -> none  [dot(): lax.dot_general(a, b, dims, precision=HIGHEST, preferred_element_type=jnp...]
    pallas_call x0 -> x1, Pallas kernels: none -> 1.94 us  [pack(): pl.pallas_call(pack_kernel, out_shape=jax.ShapeDtypeStruct((far, SUBS, ea...]
where the time goes in v3:
time: 108 us
  blocking collectives  38.5 us (36%)
  waiting for transfers between devices  30.2 us (28%)
  Pallas kernels  25 us (23%)
  starting transfers between devices  9.45 us (9%)
  local copies, waits for them, and re-layouts  3.91 us (4%)
    all_to_all x1, blocking collectives, sum_everywhere(): piece = jnp.sum(lax.all_to_all(pieces, FAR, 0, 0, tiled=True), axis=0)  30.8 us
    pallas_call x1, Pallas kernels, solve(): pl.pallas_call(functools.partial(solve_kernel, voxels), out_shape=jax.Sha...  23.1 us
    all_to_all x1, waiting for transfers between devices, sum_everywhere(): return lax.all_to_all(copies, FAR, 0, 0, tiled=True)  16 us
    all_to_all x1, waiting for transfers between devices, body(): cols = lax.all_to_all(columns, 'panel', 1, 0, tiled=True)  14.2 us
    all_to_all x1, blocking collectives, sum_everywhere(): piece = jnp.sum(lax.all_to_all(copies, NEAR, 0, 0, tiled=True), axis=0)  7.69 us
    all_to_all x1, starting transfers between devices, sum_everywhere(): return lax.all_to_all(copies, FAR, 0, 0, tiled=True)  5.15 us
    all_to_all x1, starting transfers between devices, body(): cols = lax.all_to_all(columns, 'panel', 1, 0, tiled=True)  4.29 us
    all_to_all x1, local copies, waits for them, and re-layouts, body(): cols = lax.all_to_all(columns, 'panel', 1, 0, tiled=True)  2.33 us
  transfers between devices with their start and end apart: 2, of which 2 were waited for; matrix products, arithmetic and copies ran while one was open for 0% of the time, Pallas kernels for 0%

profile of v3, /device:TPU:8, one launch (start us, length us, event | category | flops | bytes accessed | tf_op | source)
XLA Modules:
  0.0 107.5 jit_solution(5274638070116993684)
XLA Ops:
  0.0 2.3 %copy.14 = f32[8,4,8,1024]{3,2,0,1:T(8,128)} copy(f32[8,4,8,1024]{3,2,1,0:T(8,128)} %bitcast.11) | data formatting | bytes 2097152 | tf_op jit(solution)/shard_map/all_to_all | solution.py:184
  2.3 4.3 %all-to-all-start = ((f32[64,4,1024]{2,0,1:T(8,128)}), f32[64,4,1024]{2,0,1:T(8,128)S(1)}, u32[]{:S(2)}, u32[]{:S(2)}) async-start(f32[64,4,1024]{2,0,1:T(8,128)} %bitcast.7), calls=%async_computation | async-start | bytes 2097152 | tf_op jit(solution)/shard_map/all_to_all | solution.py:184
  6.6 0.0 copy-start.1
  6.6 0.7 copy-done.1
  7.3 0.2 compare_reduce_fusion
  7.5 14.2 %all-to-all-done = f32[64,4,1024]{2,0,1:T(8,128)S(1)} async-done(((f32[64,4,1024]{2,0,1:T(8,128)}), f32[64,4,1024]{2,0,1:T(8,128)S(1)}, u32[]{:S(2)}, u32[]{:S(2)}) %all-to-all-start) | async-done | bytes 1048608 | tf_op jit(solution)/shard_map/all_to_all | solution.py:184
  21.7 1.9 %pack.1 = f32[64,2,640]{2,1,0:T(2,128)S(1)} custom-call(f32[256,1024]{1,0:T(8,128)S(1)} %bitcast.8, f32[1,1024]{1,0:T(1,128)S(1)} %bitcast.10), custom_call_target="tpu_custom_call" | custom-call | tf_op jit(solution)/shard_map/pack/pallas_call | solution.py:95
  23.7 30.8 %all_to_all.34 = f32[64,2,640]{2,1,0:T(2,128)S(1)} all-to-all(f32[64,2,640]{2,1,0:T(2,128)S(1)} %pack.1), channel_id=1, replica_groups=mesh['z'=8,'y'=8,'core'=2,'panel'=4] {'z','y'}, dimensions={0} | all-to-all | bytes 655360 | tf_op jit(solution)/shard_map/all_to_all | solution.py:173
  54.5 0.1 reduce_sum.18
  54.7 7.7 %all_to_all.35 = f32[8,2,640]{2,1,0:T(2,128)S(1)} all-to-all(f32[8,2,640]{2,1,0:T(2,128)S(1)} %broadcast_in_dim.4), channel_id=1, replica_groups=mesh['z'=8,'y'=8,'core'=2,'panel'=4] {'core','panel'}, dimensions={0} | all-to-all | bytes 81920 | tf_op jit(solution)/shard_map/all_to_all | solution.py:175
  62.4 0.8 broadcast_in_dim.5
  63.2 0.0 copy-start
  63.2 5.2 %all-to-all-start.3 = ((f32[64,2,640]{2,1,0:T(2,128)}), f32[64,2,640]{2,1,0:T(2,128)S(1)}, u32[]{:S(2)}, u32[]{:S(2)}) async-start(f32[64,2,640]{2,1,0:T(2,128)} %broadcast_in_dim.5), calls=%async_computation.3 | async-start | bytes 655360 | tf_op jit(solution)/shard_map/all_to_all | solution.py:177
  68.3 0.0 copy-done
  68.3 0.1 copy.10.start_ref
  68.4 16.0 %all-to-all-done.3.packed_ref = f32[64,2,640]{2,1,0:T(2,128)S(1)} async-done(((f32[64,2,640]{2,1,0:T(2,128)}), f32[64,2,640]{2,1,0:T(2,128)S(1)}, u32[]{:S(2)}, u32[]{:S(2)}) %all-to-all-start.3) | async-done | bytes 327712 | tf_op jit(solution)/shard_map/all_to_all | solution.py:177
  84.5 23.1 %solve.1 = f32[32,1024]{1,0:T(8,128)} custom-call(f32[64,2,640]{2,1,0:T(2,128)S(1)} %all-to-all-done.3.packed_ref, f32[256,32]{1,0:T(8,128)S(1)} %copy.10.start_ref, f32[256,1024]{1,0:T(8,128)S(1)} %bitcast.9), custom_call_target="tpu_custom_call" | custom-call | tf_op jit(solution)/shard_map/solve/pallas_call | solution.py:159
  (4 shorter events, 0.0 us)
Async XLA Ops:
  2.3 19.4 %all-to-all-start = ((f32[64,4,1024]{2,0,1:T(8,128)}), f32[64,4,1024]{2,0,1:T(8,128)S(1)}, u32[]{:S(2)}, u32[]{:S(2)}) async-start(f32[64,4,1024]{2,0,1:T(8,128)} %bitcast.7), calls=%async_computation | async-start | bytes 2097152 | tf_op jit(solution)/shard_map/all_to_all | solution.py:184
  6.6 0.7 copy-start.1
  63.2 5.2 %copy-start = (f32[256,32]{0,1:T(8,128)S(1)}, f32[256,32]{0,1:T(8,128)}, u32[]{:S(2)}) copy-start(f32[256,32]{0,1:T(8,128)} %param.5) | copy-start | bytes 98308
  63.2 21.3 %all-to-all-start.3 = ((f32[64,2,640]{2,1,0:T(2,128)}), f32[64,2,640]{2,1,0:T(2,128)S(1)}, u32[]{:S(2)}, u32[]{:S(2)}) async-start(f32[64,2,640]{2,1,0:T(2,128)} %broadcast_in_dim.5), calls=%async_computation.3 | async-start | bytes 655360 | tf_op jit(solution)/shard_map/all_to_all | solution.py:177

commit v4 on v3

v4 whole, which is shorter than its diff:
```python
import functools

import jax
import jax.numpy as jnp
from jax import lax
from jax.experimental import pallas as pl
from jax.experimental.pallas import tpu as pltpu
from jax.sharding import Mesh, PartitionSpec as P

ITERS = 3
CORE_SHIFT = 0.1
HIGHEST = lax.Precision.HIGHEST
SUB = 8
LANES = 128
BLOCK = 32
SUBS = 2

FAR = ("z", "y")
NEAR = ("core", "panel")
ROWS = ("z", "y", "core")


ROWS_BY_COLS = (((1,), (0,)), ((), ()))
ROWS_BY_ROWS = (((1,), (1,)), ((), ()))
COLS_BY_COLS = (((0,), (0,)), ((), ()))

LEFT = (0, 0, 1, 0, 2, 1)
RIGHT = (0, 1, 0, 2, 0, 1)


def dot(a, b, dims=ROWS_BY_COLS):
    return lax.dot_general(a, b, dims, precision=HIGHEST, preferred_element_type=jnp.float32)


def split(x):
    first = x.astype(jnp.bfloat16)
    rest = x - first.astype(jnp.float32)
    second = rest.astype(jnp.bfloat16)
    return first, second, (rest - second.astype(jnp.float32)).astype(jnp.bfloat16)


def stack_rows(x, order):
    parts = split(x)
    return jnp.concatenate([parts[i] for i in order], axis=0)


def by_parts(x, parts):
    n = x.shape[0]
    lhs = jnp.concatenate(split(x), axis=0)
    r0 = jnp.dot(lhs, parts[0], preferred_element_type=jnp.float32)
    r1 = jnp.dot(lhs[: 2 * n], parts[1], preferred_element_type=jnp.float32)
    r2 = jnp.dot(lhs[:n], parts[2], preferred_element_type=jnp.float32)
    return r0[:n] + ((r0[n : 2 * n] + r1[:n]) + (r0[2 * n :] + r1[n:] + r2))


def by_factor(factor, x):
    size = x.shape[0]
    first, second, third = [t.astype(jnp.float32) for t in split(factor)]
    group = lax.broadcasted_iota(jnp.int32, factor.shape, 1) // size
    left = jnp.where(group == 2, second, first)
    right = jnp.where(group == 0, third, second)
    lhs = jnp.concatenate([left, right[:, : 2 * size]], axis=1).astype(jnp.bfloat16)
    return jnp.dot(lhs, stack_rows(x, RIGHT), preferred_element_type=jnp.float32)


def outer_square(x):
    return lax.dot_general(
        stack_rows(x, LEFT), stack_rows(x, RIGHT), COLS_BY_COLS, preferred_element_type=jnp.float32
    )


def inverse_factor(square, size):
    blocks = size // SUB
    row = lax.broadcasted_iota(jnp.int32, (SUB, LANES), 0)
    lane = lax.broadcasted_iota(jnp.int32, (SUB, LANES), 1)

    def spread(tile, r):
        return jnp.broadcast_to(tile[r : r + 1, :], (SUB, LANES))

    cols = [[None] * blocks for _ in range(size)]
    for j in range(size):
        for q in range(j // SUB, blocks):
            cols[j][q] = jnp.broadcast_to(square[SUB * q : SUB * q + SUB, j : j + 1], (SUB, LANES))
    inv = [jnp.where(lane % size == row + SUB * q, 1.0, 0.0) for q in range(blocks)]
    pivots = [jnp.zeros((SUB, LANES), jnp.float32) for _ in range(blocks)]
    for k in range(size):
        kq, kr = divmod(k, SUB)
        pivot = spread(cols[k][kq], kr)
        recip = pl.reciprocal(pivot, approx=True)
        recip = recip * (2.0 - pivot * recip)
        pivots[kq] = jnp.where(row == kr, pivot, pivots[kq])
        lower = list(cols[k])
        lower[kq] = jnp.where(row > kr, cols[k][kq], 0.0)
        lower = [None if t is None else t * recip for t in lower]
        for j in range(k + 1, size):
            jq, jr = divmod(j, SUB)
            factor = spread(cols[k][jq], jr)
            for q in range(jq, blocks):
                cols[j][q] = cols[j][q] - lower[q] * factor
        above = spread(inv[kq], kr)
        for q in range(kq, blocks):
            inv[q] = inv[q] - lower[q] * above
    return jnp.concatenate([t * lax.rsqrt(p) for t, p in zip(inv, pivots)], axis=0)


def pack_kernel(cols_ref, chosen_ref, out_ref):
    far, subs, width = out_ref.shape
    size = cols_ref.shape[0]
    each = size // far // subs
    cols = cols_ref[...]
    picked = cols * chosen_ref[...]
    gram = dot(cols, cols, ROWS_BY_ROWS)
    core = dot(picked, cols, ROWS_BY_ROWS)
    row = lax.broadcasted_iota(jnp.int32, (size, size), 0)
    lane = lax.broadcasted_iota(jnp.int32, (size, size), 1)
    packed = jnp.where(row >= lane, gram, core)
    diagonal = jnp.sum(jnp.where(row == lane, core, 0.0), axis=1, keepdims=True)
    spare = width - each * size
    spare_lane = lax.broadcasted_iota(jnp.int32, (far, spare), 1)
    for r in range(subs):
        tail = jnp.zeros((far, spare), jnp.float32)
        for h in range(each):
            first = (r * each + h) * far
            out_ref[:, r, h * size : (h + 1) * size] = packed[first : first + far, :]
            tail = jnp.where(spare_lane == h, diagonal[first : first + far, :], tail)
        out_ref[:, r, each * size :] = tail


def pack(cols, chosen, far):
    size = cols.shape[0]
    each = size // far // SUBS
    return pl.pallas_call(
        pack_kernel,
        out_shape=jax.ShapeDtypeStruct((far, SUBS, each * size + LANES), jnp.float32),
        in_specs=[pl.BlockSpec(memory_space=pltpu.VMEM)] * 2,
        out_specs=pl.BlockSpec(memory_space=pltpu.VMEM),
        compiler_params=pltpu.CompilerParams(vmem_limit_bytes=32 * 2**20),
        name="pack",
    )(cols, chosen)


def solve_kernel(voxels, packed_ref, start_ref, cols_ref, out_ref, work, basis, gram_parts, inverse_parts):
    size = cols_ref.shape[0]
    rank = start_ref.shape[0]
    far, subs, width = packed_ref.shape
    each = size // far // subs
    every_row = lax.broadcasted_iota(jnp.int32, (size, size), 0)
    every_lane = lax.broadcasted_iota(jnp.int32, (size, size), 1)
    rows, diagonal = [], []
    for r in range(subs):
        tail = packed_ref[:, r, each * size :]
        for h in range(each):
            rows.append(packed_ref[:, r, h * size : (h + 1) * size])
            diagonal.append(tail[:, h : h + 1])
    packed = jnp.concatenate(rows, axis=0)
    flipped = packed.T
    for i, part in enumerate(split(jnp.where(every_row >= every_lane, packed, flipped) * (1.0 / voxels))):
        gram_parts[i] = part
    core = jnp.where(every_row < every_lane, packed, flipped)
    core = jnp.where(every_row == every_lane, jnp.concatenate(diagonal, axis=0), core) * (1.0 / size)
    core = core + jnp.where(every_row == every_lane, CORE_SHIFT, 0.0)
    work[...] = core

    lane = lax.broadcasted_iota(jnp.int32, (BLOCK, size), 1)
    row = lax.broadcasted_iota(jnp.int32, (BLOCK, size), 0)

    def update(scaled, base):
        keep_row = (every_row < base) | (every_row >= base + BLOCK)
        keep_lane = (every_lane < base) | (every_lane >= base + BLOCK)
        work[...] = jnp.where(keep_row & keep_lane, work[...], 0.0) - outer_square(scaled)

    def sweep(step, carry):
        scaled, corner = carry
        base = step * BLOCK
        factor = inverse_factor(corner, BLOCK)
        update(scaled, base - BLOCK)
        band = work[pl.ds(pl.multiple_of(base, BLOCK), BLOCK), :]
        inside = (lane >= base) & (lane < base + BLOCK)
        band = jnp.where(inside, jnp.where(lane - base == row, -1.0, 0.0), band)
        scaled = by_factor(factor, band)
        then = jnp.minimum(base + BLOCK, size - BLOCK)
        tile = pl.multiple_of(then // LANES * LANES, LANES)
        corner = work[pl.ds(pl.multiple_of(then, BLOCK), BLOCK), pl.ds(tile, LANES)]
        own = scaled[:, :LANES]
        for t in range(LANES, size, LANES):
            own = jnp.where(then >= t, scaled[:, t : t + LANES], own)
        shift = LANES - lax.rem(then, LANES)
        own = pltpu.roll(own, shift, axis=1)
        corner = pltpu.roll(corner, shift, axis=1) - outer_square(own)[:BLOCK, :]
        return scaled, corner

    nothing = jnp.zeros((BLOCK, size), jnp.float32)
    scaled, _ = lax.fori_loop(0, size // BLOCK, sweep, (nothing, core[:BLOCK, :LANES]))
    update(scaled, size - BLOCK)
    for i, part in enumerate(split(-work[...])):
        inverse_parts[i] = part

    def by(ref, x):
        return by_parts(x, (ref[0], ref[1], ref[2]))

    def iterate(step, carry):
        image, pushed = carry
        small = dot(image, pushed, ROWS_BY_ROWS)
        small = jnp.concatenate([small, jnp.zeros((rank, LANES - rank), jnp.float32)], axis=1)
        factor = inverse_factor(small, rank)
        top = jnp.max(jnp.max(jnp.abs(pushed), axis=0, keepdims=True), axis=1, keepdims=True)
        ahead = by(inverse_parts, pushed * (1.0 / top))
        ahead_pushed = by(gram_parts, ahead)
        basis[...] = by_factor(factor, image)
        scaled_factor = factor * top
        return by_factor(scaled_factor, ahead), by_factor(scaled_factor, ahead_pushed)

    image = by(inverse_parts, by(gram_parts, start_ref[...]))
    lax.fori_loop(0, ITERS, iterate, (image, by(gram_parts, image)))
    out_ref[...] = dot(basis[...], cols_ref[...])


def solve(packed, start, cols, voxels):
    size, width = cols.shape
    return pl.pallas_call(
        functools.partial(solve_kernel, voxels),
        out_shape=jax.ShapeDtypeStruct((start.shape[0], width), jnp.float32),
        in_specs=[pl.BlockSpec(memory_space=pltpu.VMEM)] * 3,
        out_specs=pl.BlockSpec(memory_space=pltpu.VMEM),
        scratch_shapes=[
            pltpu.VMEM((size, size), jnp.float32),
            pltpu.VMEM(start.shape, jnp.float32),
            pltpu.VMEM((3, size, size), jnp.bfloat16),
            pltpu.VMEM((3, size, size), jnp.bfloat16),
        ],
        compiler_params=pltpu.CompilerParams(vmem_limit_bytes=32 * 2**20),
        name="solve",
    )(packed, start, cols)


def sum_everywhere(pieces):
    far, subs, width = pieces.shape
    near = lax.axis_size(NEAR)
    piece = jnp.sum(lax.all_to_all(pieces, FAR, 0, 0, tiled=True), axis=0)
    copies = jnp.broadcast_to(piece[None], (near, subs, width))
    piece = jnp.sum(lax.all_to_all(copies, NEAR, 0, 0, tiled=True), axis=0)
    copies = jnp.broadcast_to(piece[None], (far, subs, width))
    return lax.all_to_all(copies, FAR, 0, 0, tiled=True)


def body(columns, pivots, start):
    width = columns.shape[1] // lax.axis_size("panel")
    place = lax.axis_index(ROWS + ("panel",))
    voxels = width * lax.axis_size(ROWS + ("panel",))
    cols = lax.all_to_all(columns, "panel", 1, 0, tiled=True)
    here = jnp.arange(width, dtype=jnp.int32) + place * width
    chosen = jnp.any(pivots[:, None] == here[None, :], axis=0, keepdims=True).astype(jnp.float32)
    packed = sum_everywhere(pack(cols, chosen, lax.axis_size(FAR)))
    return solve(packed, start.T, cols, voxels)


def solution(mesh):
    fine = Mesh(mesh.devices.reshape(8, 8, 2, 4), ROWS + ("panel",))
    return jax.shard_map(
        body,
        mesh=fine,
        in_specs=(P("panel", ROWS), P(), P()),
        out_specs=P(None, ROWS + ("panel",)),
        check_vma=False,
    )
```

time: 108 us -> 97.2 us (0.900)
  blocking collectives: 38.5 us -> 58.9 us
  waiting for transfers between devices: 30.2 us -> 14.2 us
  Pallas kernels: 25 us -> 15.9 us
  starting transfers between devices: 9.45 us -> 4.29 us
    all_to_all x0 -> x1, blocking collectives: none -> 20.4 us  [sum_everywhere(): return lax.all_to_all(copies, FAR, 0, 0, tiled=True)]
    all_to_all x1 -> x0, waiting for transfers between devices: 16 us -> none  [sum_everywhere(): return lax.all_to_all(copies, FAR, 0, 0, tiled=True)]
    pallas_call x1, Pallas kernels: 23.1 us -> 13.9 us  [solve(): pl.pallas_call(functools.partial(solve_kernel, voxels), out_shape=jax.Sha...]
    all_to_all x1 -> x0, starting transfers between devices: 5.15 us -> none  [sum_everywhere(): return lax.all_to_all(copies, FAR, 0, 0, tiled=True)]
  transfers between devices with their start and end apart: 2 -> 1, of which waited for: 2 -> 1; matrix products, arithmetic and copies ran while one was open for 0% -> 0% of each run, Pallas kernels for 0% -> 0%
where the time goes in v4:
time: 97.2 us; the launch traced here: 96.8 us
  blocking collectives  58.9 us (61%)
  Pallas kernels  15.9 us (16%)
  waiting for transfers between devices  14.2 us (15%)
  starting transfers between devices  4.29 us (4%)
  local copies, waits for them, and re-layouts  3.11 us (3%)
    all_to_all x1, blocking collectives, sum_everywhere(): piece = jnp.sum(lax.all_to_all(pieces, FAR, 0, 0, tiled=True), axis=0)  30.8 us
    all_to_all x1, blocking collectives, sum_everywhere(): return lax.all_to_all(copies, FAR, 0, 0, tiled=True)  20.4 us
    all_to_all x1, waiting for transfers between devices, body(): cols = lax.all_to_all(columns, 'panel', 1, 0, tiled=True)  14.2 us
    pallas_call x1, Pallas kernels, solve(): pl.pallas_call(functools.partial(solve_kernel, voxels), out_shape=jax.Sha...  13.9 us
    all_to_all x1, blocking collectives, sum_everywhere(): piece = jnp.sum(lax.all_to_all(copies, NEAR, 0, 0, tiled=True), axis=0)  7.69 us
    all_to_all x1, starting transfers between devices, body(): cols = lax.all_to_all(columns, 'panel', 1, 0, tiled=True)  4.29 us
    all_to_all x1, local copies, waits for them, and re-layouts, body(): cols = lax.all_to_all(columns, 'panel', 1, 0, tiled=True)  2.33 us
  transfers between devices with their start and end apart: 1, of which 1 were waited for; matrix products, arithmetic and copies ran while one was open for 0% of the time, Pallas kernels for 0%

profile of v4, /device:TPU:8, one launch (start us, length us, event | category | flops | bytes accessed | tf_op | source)
XLA Modules:
  0.0 96.8 jit_solution(17204110717514585833)
XLA Ops:
  0.0 2.3 %copy.11 = f32[8,4,8,1024]{3,2,0,1:T(8,128)} copy(f32[8,4,8,1024]{3,2,1,0:T(8,128)} %bitcast.13) | data formatting | bytes 2097152 | tf_op jit(solution)/shard_map/all_to_all | solution.py:250
  2.3 4.3 %all-to-all-start = ((f32[64,4,1024]{2,0,1:T(8,128)}), f32[64,4,1024]{2,0,1:T(8,128)S(1)}, u32[]{:S(2)}, u32[]{:S(2)}) async-start(f32[64,4,1024]{2,0,1:T(8,128)} %bitcast.8), calls=%async_computation | async-start | bytes 2097152 | tf_op jit(solution)/shard_map/all_to_all | solution.py:250
  6.6 0.0 copy-start.1
  6.6 0.7 copy-done.1
  7.3 0.2 compare_reduce_fusion
  7.5 14.2 %all-to-all-done = f32[64,4,1024]{2,0,1:T(8,128)S(1)} async-done(((f32[64,4,1024]{2,0,1:T(8,128)}), f32[64,4,1024]{2,0,1:T(8,128)S(1)}, u32[]{:S(2)}, u32[]{:S(2)}) %all-to-all-start) | async-done | bytes 1048608 | tf_op jit(solution)/shard_map/all_to_all | solution.py:250
  21.7 1.9 %pack.1 = f32[64,2,640]{2,1,0:T(2,128)S(1)} custom-call(f32[256,1024]{1,0:T(8,128)S(1)} %bitcast.9, f32[1,1024]{1,0:T(1,128)S(1)} %bitcast.12), custom_call_target="tpu_custom_call" | custom-call | tf_op jit(solution)/shard_map/pack/pallas_call | solution.py:132
  23.7 30.8 %all_to_all.34 = f32[64,2,640]{2,1,0:T(2,128)S(1)} all-to-all(f32[64,2,640]{2,1,0:T(2,128)S(1)} %pack.1), channel_id=1, replica_groups=mesh['z'=8,'y'=8,'core'=2,'panel'=4] {'z','y'}, dimensions={0} | all-to-all | bytes 655360 | tf_op jit(solution)/shard_map/all_to_all | solution.py:239
  54.5 0.1 reduce_sum.18
  54.7 7.7 %all_to_all.35 = f32[8,2,640]{2,1,0:T(2,128)S(1)} all-to-all(f32[8,2,640]{2,1,0:T(2,128)S(1)} %broadcast_in_dim.4), channel_id=1, replica_groups=mesh['z'=8,'y'=8,'core'=2,'panel'=4] {'core','panel'}, dimensions={0} | all-to-all | bytes 81920 | tf_op jit(solution)/shard_map/all_to_all | solution.py:241
  62.4 0.1 broadcast_in_dim.5
  62.5 0.0 copy-start
  62.5 20.4 %all_to_all.36.packed_ref = f32[64,2,640]{2,1,0:T(2,128)S(1)} all-to-all(f32[64,2,640]{2,1,0:T(2,128)S(1)} %broadcast_in_dim.5), channel_id=1, replica_groups=mesh['z'=8,'y'=8,'core'=2,'panel'=4] {'z','y'}, dimensions={0} | all-to-all | bytes 655360 | tf_op jit(solution)/shard_map/all_to_all | solution.py:243
  82.9 0.0 copy-done
  82.9 13.9 %solve.1 = f32[32,1024]{1,0:T(8,128)} custom-call(f32[64,2,640]{2,1,0:T(2,128)S(1)} %all_to_all.36.packed_ref, f32[32,256]{1,0:T(8,128)S(1)} %bitcast.11, f32[256,1024]{1,0:T(8,128)S(1)} %bitcast.10), custom_call_target="tpu_custom_call" | custom-call | tf_op jit(solution)/shard_map/solve/pallas_call | solution.py:220
  (4 shorter events, 0.0 us)
Async XLA Ops:
  2.3 19.4 %all-to-all-start = ((f32[64,4,1024]{2,0,1:T(8,128)}), f32[64,4,1024]{2,0,1:T(8,128)S(1)}, u32[]{:S(2)}, u32[]{:S(2)}) async-start(f32[64,4,1024]{2,0,1:T(8,128)} %bitcast.8), calls=%async_computation | async-start | bytes 2097152 | tf_op jit(solution)/shard_map/all_to_all | solution.py:250
  6.6 0.7 copy-start.1
  62.5 20.4 %copy-start = (f32[256,32]{0,1:T(8,128)S(1)}, f32[256,32]{0,1:T(8,128)}, u32[]{:S(2)}) copy-start(f32[256,32]{0,1:T(8,128)} %param.5) | copy-start | bytes 98308

commit v5 on v4

--- a/solution.py
+++ b/solution.py
@@ -13,10 +13,11 @@
 SUB = 8
 LANES = 128
 BLOCK = 32
-SUBS = 2
-
-FAR = ("z", "y")
-NEAR = ("core", "panel")
+PANEL = 16
+SUBS = 4
+
+FAR = ("panel", "y")
+NEAR = ("z", "core")
 ROWS = ("z", "y", "core")
 
 
@@ -57,15 +58,15 @@
     size = x.shape[0]
     first, second, third = [t.astype(jnp.float32) for t in split(factor)]
     group = lax.broadcasted_iota(jnp.int32, factor.shape, 1) // size
-    left = jnp.where(group == 2, second, first)
-    right = jnp.where(group == 0, third, second)
-    lhs = jnp.concatenate([left, right[:, : 2 * size]], axis=1).astype(jnp.bfloat16)
-    return jnp.dot(lhs, stack_rows(x, RIGHT), preferred_element_type=jnp.float32)
-
-
-def outer_square(x):
+    left = jnp.where(group == 0, 0.0, jnp.where(group == 3, second, first))
+    right = jnp.where(group == 0, 0.0, jnp.where(group == 3, second, jnp.where(group == 2, third, first)))
+    lhs = jnp.concatenate([left, right], axis=1).astype(jnp.bfloat16)
+    return jnp.dot(lhs, stack_rows(x, (0, 0, 1, 0, 0, 2, 0, 1)), preferred_element_type=jnp.float32)
+
+
+def by_columns(x, y):
     return lax.dot_general(
-        stack_rows(x, LEFT), stack_rows(x, RIGHT), COLS_BY_COLS, preferred_element_type=jnp.float32
+        stack_rows(x, LEFT), stack_rows(y, RIGHT), COLS_BY_COLS, preferred_element_type=jnp.float32
     )
 
 
@@ -77,52 +78,71 @@
     def spread(tile, r):
         return jnp.broadcast_to(tile[r : r + 1, :], (SUB, LANES))
 
-    cols = [[None] * blocks for _ in range(size)]
-    for j in range(size):
-        for q in range(j // SUB, blocks):
-            cols[j][q] = jnp.broadcast_to(square[SUB * q : SUB * q + SUB, j : j + 1], (SUB, LANES))
-    inv = [jnp.where(lane % size == row + SUB * q, 1.0, 0.0) for q in range(blocks)]
+    rows = []
+    for q in range(blocks):
+        unit = jnp.where(lane % size == row + SUB * q, 1.0, 0.0)
+        rows.append(jnp.where(lane < size, square[SUB * q : SUB * q + SUB, :], unit))
     pivots = [jnp.zeros((SUB, LANES), jnp.float32) for _ in range(blocks)]
-    for k in range(size):
-        kq, kr = divmod(k, SUB)
-        pivot = spread(cols[k][kq], kr)
-        recip = pl.reciprocal(pivot, approx=True)
-        recip = recip * (2.0 - pivot * recip)
-        pivots[kq] = jnp.where(row == kr, pivot, pivots[kq])
-        lower = list(cols[k])
-        lower[kq] = jnp.where(row > kr, cols[k][kq], 0.0)
-        lower = [None if t is None else t * recip for t in lower]
-        for j in range(k + 1, size):
-            jq, jr = divmod(j, SUB)
-            factor = spread(cols[k][jq], jr)
-            for q in range(jq, blocks):
-                cols[j][q] = cols[j][q] - lower[q] * factor
-        above = spread(inv[kq], kr)
-        for q in range(kq, blocks):
-            inv[q] = inv[q] - lower[q] * above
-    return jnp.concatenate([t * lax.rsqrt(p) for t, p in zip(inv, pivots)], axis=0)
+    for first in range(0, size, PANEL):
+        last = first + PANEL - 1
+        cols = {}
+        for j in range(first, last + 1):
+            for q in range(j // SUB, blocks):
+                cols[j, q] = jnp.broadcast_to(rows[q][:, j : j + 1], (SUB, LANES))
+        pivot = spread(cols[first, first // SUB], first % SUB)
+        for k in range(first, last + 1):
+            kq, kr = divmod(k, SUB)
+            rough = pl.reciprocal(pivot, approx=True)
+            fix = 2.0 - pivot * rough
+            recip = rough * fix
+            pivots[kq] = jnp.where(row == kr, pivot, pivots[kq])
+            if k < last:
+                nq, nr = divmod(k + 1, SUB)
+                beside = spread(cols[k, nq], nr)
+                pivot = spread(cols[k + 1, nq], nr) - (beside * beside * rough) * fix
+            lower = {q: cols[k, q] for q in range(kq, blocks)}
+            lower[kq] = jnp.where(row > kr, lower[kq], 0.0)
+            lower = {q: t * recip for q, t in lower.items()}
+            for j in range(k + 1, last + 1):
+                jq, jr = divmod(j, SUB)
+                factor = spread(cols[k, jq], jr)
+                for q in range(jq, blocks):
+                    cols[j, q] = cols[j, q] - lower[q] * factor
+            above = spread(rows[kq], kr)
+            for q in range(kq, blocks):
+                rows[q] = rows[q] - lower[q] * above
+    return jnp.concatenate([t * lax.rsqrt(p) for t, p in zip(rows, pivots)], axis=0)
 
 
 def pack_kernel(cols_ref, chosen_ref, out_ref):
     far, subs, width = out_ref.shape
     size = cols_ref.shape[0]
     each = size // far // subs
-    cols = cols_ref[...]
-    picked = cols * chosen_ref[...]
-    gram = dot(cols, cols, ROWS_BY_ROWS)
-    core = dot(picked, cols, ROWS_BY_ROWS)
     row = lax.broadcasted_iota(jnp.int32, (size, size), 0)
     lane = lax.broadcasted_iota(jnp.int32, (size, size), 1)
-    packed = jnp.where(row >= lane, gram, core)
-    diagonal = jnp.sum(jnp.where(row == lane, core, 0.0), axis=1, keepdims=True)
+    high, middle, low = split(cols_ref[...])
+    chosen = chosen_ref[...].astype(jnp.bfloat16)
+    first = jnp.concatenate([high, high * chosen], axis=0)
+    second = jnp.concatenate([middle, middle * chosen], axis=0)
+
+    def product(x, y):
+        return lax.dot_general(x, y, ROWS_BY_ROWS, preferred_element_type=jnp.float32)
+
+    mirrored = product(first, low) + product(first, middle)
+    plain = product(second, middle) + product(first, high)
+    gram_half, core_half = mirrored[:size], mirrored[size:]
+    turned = jnp.where(row <= lane, gram_half, core_half).T
+    packed = jnp.where(row >= lane, plain[:size] + gram_half, plain[size:] + core_half) + turned
+    core_diagonal = plain[size:] + 2.0 * core_half
+    diagonal = jnp.sum(jnp.where(row == lane, core_diagonal, 0.0), axis=1, keepdims=True)
     spare = width - each * size
     spare_lane = lax.broadcasted_iota(jnp.int32, (far, spare), 1)
     for r in range(subs):
         tail = jnp.zeros((far, spare), jnp.float32)
         for h in range(each):
-            first = (r * each + h) * far
-            out_ref[:, r, h * size : (h + 1) * size] = packed[first : first + far, :]
-            tail = jnp.where(spare_lane == h, diagonal[first : first + far, :], tail)
+            at = (r * each + h) * far
+            out_ref[:, r, h * size : (h + 1) * size] = packed[at : at + far, :]
+            tail = jnp.where(spare_lane == h, diagonal[at : at + far, :], tail)
         out_ref[:, r, each * size :] = tail
 
 
@@ -139,7 +159,7 @@
     )(cols, chosen)
 
 
-def solve_kernel(voxels, packed_ref, start_ref, cols_ref, out_ref, work, basis, gram_parts, inverse_parts):
+def solve_kernel(voxels, packed_ref, start_ref, cols_ref, out_ref, work, gram, basis, gram_parts, inverse_parts, cols_parts):
     size = cols_ref.shape[0]
     rank = start_ref.shape[0]
     far, subs, width = packed_ref.shape
@@ -154,8 +174,7 @@
             diagonal.append(tail[:, h : h + 1])
     packed = jnp.concatenate(rows, axis=0)
     flipped = packed.T
-    for i, part in enumerate(split(jnp.where(every_row >= every_lane, packed, flipped) * (1.0 / voxels))):
-        gram_parts[i] = part
+    gram[...] = jnp.where(every_row >= every_lane, packed, flipped) * (1.0 / voxels)
     core = jnp.where(every_row < every_lane, packed, flipped)
     core = jnp.where(every_row == every_lane, jnp.concatenate(diagonal, axis=0), core) * (1.0 / size)
     core = core + jnp.where(every_row == every_lane, CORE_SHIFT, 0.0)
@@ -167,26 +186,32 @@
     def update(scaled, base):
         keep_row = (every_row < base) | (every_row >= base + BLOCK)
         keep_lane = (every_lane < base) | (every_lane >= base + BLOCK)
-        work[...] = jnp.where(keep_row & keep_lane, work[...], 0.0) - outer_square(scaled)
+        work[...] = jnp.where(keep_row & keep_lane, work[...], 0.0) - by_columns(scaled, scaled)
 
     def sweep(step, carry):
         scaled, corner = carry
-        base = step * BLOCK
+        base = pl.multiple_of(step * BLOCK, BLOCK)
+        rows_here = pl.ds(base, BLOCK)
         factor = inverse_factor(corner, BLOCK)
         update(scaled, base - BLOCK)
-        band = work[pl.ds(pl.multiple_of(base, BLOCK), BLOCK), :]
+        band = work[rows_here, :]
         inside = (lane >= base) & (lane < base + BLOCK)
         band = jnp.where(inside, jnp.where(lane - base == row, -1.0, 0.0), band)
-        scaled = by_factor(factor, band)
         then = jnp.minimum(base + BLOCK, size - BLOCK)
         tile = pl.multiple_of(then // LANES * LANES, LANES)
-        corner = work[pl.ds(pl.multiple_of(then, BLOCK), BLOCK), pl.ds(tile, LANES)]
-        own = scaled[:, :LANES]
+        shift = LANES - lax.rem(then, LANES)
+        own = band[:, :LANES]
         for t in range(LANES, size, LANES):
-            own = jnp.where(then >= t, scaled[:, t : t + LANES], own)
-        shift = LANES - lax.rem(then, LANES)
+            own = jnp.where(then >= t, band[:, t : t + LANES], own)
         own = pltpu.roll(own, shift, axis=1)
-        corner = pltpu.roll(corner, shift, axis=1) - outer_square(own)[:BLOCK, :]
+        corner = pltpu.roll(work[pl.ds(pl.multiple_of(then, BLOCK), BLOCK), pl.ds(tile, LANES)], shift, axis=1)
+        own = by_factor(factor, own)
+        corner = corner - by_columns(own, own)[:BLOCK, :]
+        scaled = by_factor(factor, band)
+        for i, part in enumerate(split(cols_ref[rows_here, :])):
+            cols_parts[i, rows_here, :] = part
+        for i, part in enumerate(split(gram[rows_here, :])):
+            gram_parts[i, rows_here, :] = part
         return scaled, corner
 
     nothing = jnp.zeros((BLOCK, size), jnp.float32)
@@ -212,21 +237,24 @@
 
     image = by(inverse_parts, by(gram_parts, start_ref[...]))
     lax.fori_loop(0, ITERS, iterate, (image, by(gram_parts, image)))
-    out_ref[...] = dot(basis[...], cols_ref[...])
+    out_ref[...] = by(cols_parts, basis[...])
 
 
 def solve(packed, start, cols, voxels):
     size, width = cols.shape
+    rank = start.shape[0]
     return pl.pallas_call(
         functools.partial(solve_kernel, voxels),
-        out_shape=jax.ShapeDtypeStruct((start.shape[0], width), jnp.float32),
+        out_shape=jax.ShapeDtypeStruct((rank, width), jnp.float32),
         in_specs=[pl.BlockSpec(memory_space=pltpu.VMEM)] * 3,
         out_specs=pl.BlockSpec(memory_space=pltpu.VMEM),
         scratch_shapes=[
             pltpu.VMEM((size, size), jnp.float32),
-            pltpu.VMEM(start.shape, jnp.float32),
+            pltpu.VMEM((size, size), jnp.float32),
+            pltpu.VMEM((rank, size), jnp.float32),
             pltpu.VMEM((3, size, size), jnp.bfloat16),
             pltpu.VMEM((3, size, size), jnp.bfloat16),
+            pltpu.VMEM((3, size, width), jnp.bfloat16),
         ],
         compiler_params=pltpu.CompilerParams(vmem_limit_bytes=32 * 2**20),
         name="solve",

time: 97.2 us -> 95.4 us (0.981)
  Pallas kernels: 15.9 us -> 14.1 us
    all_to_all x1, blocking collectives: 7.69 us -> 19.5 us  [sum_everywhere(): piece = jnp.sum(lax.all_to_all(copies, NEAR, 0, 0, tiled=True), axis=0)]
    all_to_all x1, blocking collectives: 30.8 us -> 20.6 us  [sum_everywhere(): piece = jnp.sum(lax.all_to_all(pieces, FAR, 0, 0, tiled=True), axis=0)]
    all_to_all x1, blocking collectives: 20.4 us -> 18.8 us  [sum_everywhere(): return lax.all_to_all(copies, FAR, 0, 0, tiled=True)]
    pallas_call x1, Pallas kernels: 13.9 us -> 12.6 us  [solve(): pl.pallas_call(functools.partial(solve_kernel, voxels), out_shape=jax.Sha...]
where the time goes in v5:
time: 95.4 us; the launch traced here: 95 us
  blocking collectives  58.9 us (62%)
  waiting for transfers between devices  14.2 us (15%)
  Pallas kernels  14.1 us (15%)
  starting transfers between devices  4.29 us (4%)
  local copies, waits for them, and re-layouts  3.08 us (3%)
    all_to_all x1, blocking collectives, sum_everywhere(): piece = jnp.sum(lax.all_to_all(pieces, FAR, 0, 0, tiled=True), axis=0)  20.6 us
    all_to_all x1, blocking collectives, sum_everywhere(): piece = jnp.sum(lax.all_to_all(copies, NEAR, 0, 0, tiled=True), axis=0)  19.5 us
    all_to_all x1, blocking collectives, sum_everywhere(): return lax.all_to_all(copies, FAR, 0, 0, tiled=True)  18.8 us
    all_to_all x1, waiting for transfers between devices, body(): cols = lax.all_to_all(columns, 'panel', 1, 0, tiled=True)  14.2 us
    pallas_call x1, Pallas kernels, solve(): pl.pallas_call(functools.partial(solve_kernel, voxels), out_shape=jax.Sha...  12.6 us
    all_to_all x1, starting transfers between devices, body(): cols = lax.all_to_all(columns, 'panel', 1, 0, tiled=True)  4.29 us
    all_to_all x1, local copies, waits for them, and re-layouts, body(): cols = lax.all_to_all(columns, 'panel', 1, 0, tiled=True)  2.33 us
  transfers between devices with their start and end apart: 1, of which 1 were waited for; matrix products, arithmetic and copies ran while one was open for 0% of the time, Pallas kernels for 0%

profile of v5, /device:TPU:8, one launch (start us, length us, event | category | flops | bytes accessed | tf_op | source)
XLA Modules:
  0.0 95.0 jit_solution(2763665184373427187)
XLA Ops:
  0.0 2.3 %copy.11 = f32[8,4,8,1024]{3,2,0,1:T(8,128)} copy(f32[8,4,8,1024]{3,2,1,0:T(8,128)} %bitcast.13) | data formatting | bytes 2097152 | tf_op jit(solution)/shard_map/all_to_all | solution.py:278
  2.3 4.3 %all-to-all-start = ((f32[64,4,1024]{2,0,1:T(8,128)}), f32[64,4,1024]{2,0,1:T(8,128)S(1)}, u32[]{:S(2)}, u32[]{:S(2)}) async-start(f32[64,4,1024]{2,0,1:T(8,128)} %bitcast.8), calls=%async_computation | async-start | bytes 2097152 | tf_op jit(solution)/shard_map/all_to_all | solution.py:278
  6.6 0.0 copy-start.1
  6.6 0.7 copy-done.1
  7.3 0.2 compare_reduce_fusion
  7.5 14.2 %all-to-all-done = f32[64,4,1024]{2,0,1:T(8,128)S(1)} async-done(((f32[64,4,1024]{2,0,1:T(8,128)}), f32[64,4,1024]{2,0,1:T(8,128)S(1)}, u32[]{:S(2)}, u32[]{:S(2)}) %all-to-all-start) | async-done | bytes 1048608 | tf_op jit(solution)/shard_map/all_to_all | solution.py:278
  21.7 1.5 %pack.1 = f32[32,4,640]{2,1,0:T(4,128)S(1)} custom-call(f32[256,1024]{1,0:T(8,128)S(1)} %bitcast.9, f32[1,1024]{1,0:T(1,128)S(1)} %bitcast.12), custom_call_target="tpu_custom_call" | custom-call | tf_op jit(solution)/shard_map/pack/pallas_call | solution.py:152
  23.2 20.6 %all_to_all.34 = f32[32,4,640]{2,1,0:T(4,128)S(1)} all-to-all(f32[32,4,640]{2,1,0:T(4,128)S(1)} %pack.1), channel_id=1, replica_groups=mesh['z'=8,'y'=8,'core'=2,'panel'=4] {'panel','y'}, dimensions={0} | all-to-all | bytes 655360 | tf_op jit(solution)/shard_map/all_to_all | solution.py:267
  43.8 0.1 reduce_sum.18
  43.9 19.5 %all_to_all.35 = f32[16,4,640]{2,1,0:T(4,128)S(1)} all-to-all(f32[16,4,640]{2,1,0:T(4,128)S(1)} %broadcast_in_dim.4), channel_id=1, replica_groups=mesh['z'=8,'y'=8,'core'=2,'panel'=4] {'z','core'}, dimensions={0} | all-to-all | bytes 327680 | tf_op jit(solution)/shard_map/all_to_all | solution.py:269
  63.5 0.0 copy-start
  63.5 18.8 %all_to_all.36.packed_ref = f32[32,4,640]{2,1,0:T(4,128)S(1)} all-to-all(f32[32,4,640]{2,1,0:T(4,128)S(1)} %broadcast_in_dim.5), channel_id=1, replica_groups=mesh['z'=8,'y'=8,'core'=2,'panel'=4] {'panel','y'}, dimensions={0} | all-to-all | bytes 655360 | tf_op jit(solution)/shard_map/all_to_all | solution.py:271
  82.4 0.0 copy-done
  82.4 12.6 %solve.1 = f32[32,1024]{1,0:T(8,128)} custom-call(f32[32,4,640]{2,1,0:T(4,128)S(1)} %all_to_all.36.packed_ref, f32[32,256]{1,0:T(8,128)S(1)} %bitcast.11, f32[256,1024]{1,0:T(8,128)S(1)} %bitcast.10), custom_call_target="tpu_custom_call" | custom-call | tf_op jit(solution)/shard_map/solve/pallas_call | solution.py:246
  (5 shorter events, 0.1 us)
Async XLA Ops:
  2.3 19.4 %all-to-all-start = ((f32[64,4,1024]{2,0,1:T(8,128)}), f32[64,4,1024]{2,0,1:T(8,128)S(1)}, u32[]{:S(2)}, u32[]{:S(2)}) async-start(f32[64,4,1024]{2,0,1:T(8,128)} %bitcast.8), calls=%async_computation | async-start | bytes 2097152 | tf_op jit(solution)/shard_map/all_to_all | solution.py:278
  6.6 0.7 copy-start.1
  63.5 18.9 %copy-start = (f32[256,32]{0,1:T(8,128)S(1)}, f32[256,32]{0,1:T(8,128)}, u32[]{:S(2)}) copy-start(f32[256,32]{0,1:T(8,128)} %param.5) | copy-start | bytes 98308

commit v6 on v5

--- a/solution.py
+++ b/solution.py
@@ -114,14 +114,28 @@
     return jnp.concatenate([t * lax.rsqrt(p) for t, p in zip(rows, pivots)], axis=0)
 
 
-def pack_kernel(cols_ref, chosen_ref, out_ref):
+def chosen_here(pivots_ref, width):
+    place = lax.axis_index(ROWS + ("panel",))
+    lane = lax.broadcasted_iota(jnp.int32, (LANES, LANES), 1).astype(jnp.float32)
+    chosen = []
+    for first in range(0, width, LANES):
+        chosen.append(jnp.zeros((LANES, LANES), jnp.float32))
+    for group in range(pivots_ref.shape[0]):
+        here = (pivots_ref[group : group + 1, :] - place * width).astype(jnp.float32)
+        here = jnp.broadcast_to(here, (LANES, LANES)).T
+        for i in range(len(chosen)):
+            chosen[i] = jnp.where(here == lane + float(i * LANES), 1.0, chosen[i])
+    return jnp.concatenate([jnp.max(c, axis=0, keepdims=True) for c in chosen], axis=1)
+
+
+def pack_kernel(cols_ref, pivots_ref, out_ref):
     far, subs, width = out_ref.shape
     size = cols_ref.shape[0]
     each = size // far // subs
     row = lax.broadcasted_iota(jnp.int32, (size, size), 0)
     lane = lax.broadcasted_iota(jnp.int32, (size, size), 1)
     high, middle, low = split(cols_ref[...])
-    chosen = chosen_ref[...].astype(jnp.bfloat16)
+    chosen = chosen_here(pivots_ref, cols_ref.shape[1]).astype(jnp.bfloat16)
     first = jnp.concatenate([high, high * chosen], axis=0)
     second = jnp.concatenate([middle, middle * chosen], axis=0)
 
@@ -146,7 +160,7 @@
         out_ref[:, r, each * size :] = tail
 
 
-def pack(cols, chosen, far):
+def pack(cols, pivots, far):
     size = cols.shape[0]
     each = size // far // SUBS
     return pl.pallas_call(
@@ -156,7 +170,7 @@
         out_specs=pl.BlockSpec(memory_space=pltpu.VMEM),
         compiler_params=pltpu.CompilerParams(vmem_limit_bytes=32 * 2**20),
         name="pack",
-    )(cols, chosen)
+    )(cols, pivots.reshape(-1, LANES))
 
 
 def solve_kernel(voxels, packed_ref, start_ref, cols_ref, out_ref, work, gram, basis, gram_parts, inverse_parts, cols_parts):
@@ -273,12 +287,9 @@
 
 def body(columns, pivots, start):
     width = columns.shape[1] // lax.axis_size("panel")
-    place = lax.axis_index(ROWS + ("panel",))
     voxels = width * lax.axis_size(ROWS + ("panel",))
     cols = lax.all_to_all(columns, "panel", 1, 0, tiled=True)
-    here = jnp.arange(width, dtype=jnp.int32) + place * width
-    chosen = jnp.any(pivots[:, None] == here[None, :], axis=0, keepdims=True).astype(jnp.float32)
-    packed = sum_everywhere(pack(cols, chosen, lax.axis_size(FAR)))
+    packed = sum_everywhere(pack(cols, pivots, lax.axis_size(FAR)))
     return solve(packed, start.T, cols, voxels)
 
 

time: 95.4 us -> 94.9 us (level)
  blocking collectives: 58.9 us -> 78.1 us
  waiting for transfers between devices: 14.2 us -> 0 us
  starting transfers between devices: 4.29 us -> 0 us
  local copies, waits for them, and re-layouts: 3.08 us -> 2.08 us
    all_to_all x0 -> x1, blocking collectives: none -> 19.2 us  [body(): cols = lax.all_to_all(columns, 'panel', 1, 0, tiled=True)]
    all_to_all x1 -> x0, waiting for transfers between devices: 14.2 us -> none  [body(): cols = lax.all_to_all(columns, 'panel', 1, 0, tiled=True)]
    all_to_all x1 -> x0, starting transfers between devices: 4.29 us -> none  [body(): cols = lax.all_to_all(columns, 'panel', 1, 0, tiled=True)]
    all_to_all x1, local copies, waits for them, and re-layouts: 2.33 us -> 1.32 us  [body(): cols = lax.all_to_all(columns, 'panel', 1, 0, tiled=True)]
  transfers between devices with their start and end apart: 1 -> 0, of which waited for: 1 -> 0; matrix products, arithmetic and copies ran while one was open for 0% -> 0% of each run, Pallas kernels for 0% -> 0%
where the time goes in v6:
time: 94.9 us; the launch traced here: 94.6 us
  blocking collectives  78.1 us (82%)
  Pallas kernels  14.2 us (15%)
  local copies, waits for them, and re-layouts  2.08 us (2%)
    all_to_all x1, blocking collectives, sum_everywhere(): piece = jnp.sum(lax.all_to_all(pieces, FAR, 0, 0, tiled=True), axis=0)  20.6 us
    all_to_all x1, blocking collectives, sum_everywhere(): piece = jnp.sum(lax.all_to_all(copies, NEAR, 0, 0, tiled=True), axis=0)  19.5 us
    all_to_all x1, blocking collectives, body(): cols = lax.all_to_all(columns, 'panel', 1, 0, tiled=True)  19.2 us
    all_to_all x1, blocking collectives, sum_everywhere(): return lax.all_to_all(copies, FAR, 0, 0, tiled=True)  18.8 us
    pallas_call x1, Pallas kernels, solve(): pl.pallas_call(functools.partial(solve_kernel, voxels), out_shape=jax.Sha...  12.6 us

profile of v6, /device:TPU:8, one launch (start us, length us, event | category | flops | bytes accessed | tf_op | source)
XLA Modules:
  0.0 94.6 jit_solution(6551147298283021443)
XLA Ops:
  0.0 1.3 %copy.11 = f32[8,4,8,1024]{3,2,0,1:T(8,128)S(1)} copy(f32[8,4,8,1024]{3,2,1,0:T(8,128)} %bitcast.14) | data formatting | bytes 2097152 | tf_op jit(solution)/shard_map/all_to_all | solution.py:291
  1.3 19.2 %all_to_all.34 = f32[64,4,1024]{2,0,1:T(8,128)S(1)} all-to-all(f32[64,4,1024]{2,0,1:T(8,128)S(1)} %bitcast.13), channel_id=1, replica_groups=mesh['z'=8,'y'=8,'core'=2,'panel'=4] {'panel'}, dimensions={1} | all-to-all | bytes 2097152 | tf_op jit(solution)/shard_map/all_to_all | solution.py:291
  20.5 0.0 copy-start.1
  20.5 0.7 copy-done.1
  21.2 1.6 %pack.1 = f32[32,4,640]{2,1,0:T(4,128)S(1)} custom-call(f32[256,1024]{1,0:T(8,128)S(1)} %bitcast.9, s32[2,128]{1,0:T(2,128)S(1)} %bitcast.12), custom_call_target="tpu_custom_call" | custom-call | tf_op jit(solution)/shard_map/pack/pallas_call | solution.py:166
  22.8 20.6 %all_to_all.35 = f32[32,4,640]{2,1,0:T(4,128)S(1)} all-to-all(f32[32,4,640]{2,1,0:T(4,128)S(1)} %pack.1), channel_id=1, replica_groups=mesh['z'=8,'y'=8,'core'=2,'panel'=4] {'panel','y'}, dimensions={0} | all-to-all | bytes 655360 | tf_op jit(solution)/shard_map/all_to_all | solution.py:281
  43.4 0.1 reduce_sum.18
  43.5 19.5 %all_to_all.36 = f32[16,4,640]{2,1,0:T(4,128)S(1)} all-to-all(f32[16,4,640]{2,1,0:T(4,128)S(1)} %broadcast_in_dim.4), channel_id=1, replica_groups=mesh['z'=8,'y'=8,'core'=2,'panel'=4] {'z','core'}, dimensions={0} | all-to-all | bytes 327680 | tf_op jit(solution)/shard_map/all_to_all | solution.py:283
  63.1 0.0 copy-start
  63.1 18.8 %all_to_all.37.packed_ref = f32[32,4,640]{2,1,0:T(4,128)S(1)} all-to-all(f32[32,4,640]{2,1,0:T(4,128)S(1)} %broadcast_in_dim.5), channel_id=1, replica_groups=mesh['z'=8,'y'=8,'core'=2,'panel'=4] {'panel','y'}, dimensions={0} | all-to-all | bytes 655360 | tf_op jit(solution)/shard_map/all_to_all | solution.py:285
  81.9 0.0 copy-done
  81.9 12.6 %solve.1 = f32[32,1024]{1,0:T(8,128)} custom-call(f32[32,4,640]{2,1,0:T(4,128)S(1)} %all_to_all.37.packed_ref, f32[32,256]{1,0:T(8,128)S(1)} %bitcast.11, f32[256,1024]{1,0:T(8,128)S(1)} %bitcast.10), custom_call_target="tpu_custom_call" | custom-call | tf_op jit(solution)/shard_map/solve/pallas_call | solution.py:260
  (3 shorter events, 0.1 us)
Async XLA Ops:
  20.5 0.7 copy-start.1
  63.1 18.9 %copy-start = (f32[256,32]{0,1:T(8,128)S(1)}, f32[256,32]{0,1:T(8,128)}, u32[]{:S(2)}) copy-start(f32[256,32]{0,1:T(8,128)} %param.5) | copy-start | bytes 98308

commit v7 on v6

--- a/solution.py
+++ b/solution.py
@@ -14,7 +14,8 @@
 LANES = 128
 BLOCK = 32
 PANEL = 16
-SUBS = 4
+EARLY = 4
+SUBS = 1
 
 FAR = ("panel", "y")
 NEAR = ("z", "core")
@@ -83,34 +84,41 @@
         unit = jnp.where(lane % size == row + SUB * q, 1.0, 0.0)
         rows.append(jnp.where(lane < size, square[SUB * q : SUB * q + SUB, :], unit))
     pivots = [jnp.zeros((SUB, LANES), jnp.float32) for _ in range(blocks)]
-    for first in range(0, size, PANEL):
-        last = first + PANEL - 1
-        cols = {}
-        for j in range(first, last + 1):
+    cols = {}
+
+    def take(first):
+        for j in range(first, min(first + PANEL, size)):
             for q in range(j // SUB, blocks):
                 cols[j, q] = jnp.broadcast_to(rows[q][:, j : j + 1], (SUB, LANES))
-        pivot = spread(cols[first, first // SUB], first % SUB)
-        for k in range(first, last + 1):
-            kq, kr = divmod(k, SUB)
-            rough = pl.reciprocal(pivot, approx=True)
-            fix = 2.0 - pivot * rough
-            recip = rough * fix
-            pivots[kq] = jnp.where(row == kr, pivot, pivots[kq])
-            if k < last:
-                nq, nr = divmod(k + 1, SUB)
-                beside = spread(cols[k, nq], nr)
-                pivot = spread(cols[k + 1, nq], nr) - (beside * beside * rough) * fix
-            lower = {q: cols[k, q] for q in range(kq, blocks)}
-            lower[kq] = jnp.where(row > kr, lower[kq], 0.0)
-            lower = {q: t * recip for q, t in lower.items()}
-            for j in range(k + 1, last + 1):
-                jq, jr = divmod(j, SUB)
-                factor = spread(cols[k, jq], jr)
-                for q in range(jq, blocks):
-                    cols[j, q] = cols[j, q] - lower[q] * factor
-            above = spread(rows[kq], kr)
-            for q in range(kq, blocks):
-                rows[q] = rows[q] - lower[q] * above
+
+    take(0)
+    pivot = spread(cols[0, 0], 0)
+    taken = PANEL
+    for k in range(size):
+        if k + EARLY == taken and taken < size:
+            take(taken)
+            taken += PANEL
+        kq, kr = divmod(k, SUB)
+        rough = pl.reciprocal(pivot, approx=True)
+        near_one = pivot * rough
+        recip = rough * (2.0 - near_one)
+        pivots[kq] = jnp.where(row == kr, pivot, pivots[kq])
+        if k + 1 < size:
+            nq, nr = divmod(k + 1, SUB)
+            beside = spread(cols[k, nq], nr)
+            square_rough = (beside * beside) * rough
+            pivot = spread(cols[k + 1, nq], nr) - square_rough * (2.0 - near_one)
+        lower = {q: cols[k, q] for q in range(kq, blocks)}
+        lower[kq] = jnp.where(row > kr, lower[kq], 0.0)
+        lower = {q: t * recip for q, t in lower.items()}
+        for j in range(k + 1, min(taken, size)):
+            jq, jr = divmod(j, SUB)
+            factor = spread(cols[k, jq], jr)
+            for q in range(jq, blocks):
+                cols[j, q] = cols[j, q] - lower[q] * factor
+        above = spread(rows[kq], kr)
+        for q in range(kq, blocks):
+            rows[q] = rows[q] - lower[q] * above
     return jnp.concatenate([t * lax.rsqrt(p) for t, p in zip(rows, pivots)], axis=0)
 
 

time: 94.9 us -> 92.1 us (0.970)
  blocking collectives: 78.1 us -> 75.8 us
    all_to_all x1, blocking collectives: 20.6 us -> 19.5 us  [sum_everywhere(): piece = jnp.sum(lax.all_to_all(pieces, FAR, 0, 0, tiled=True), axis=0)]
where the time goes in v7:
time: 92.1 us; the launch traced here: 91.7 us
  blocking collectives  75.8 us (82%)
  Pallas kernels  13.4 us (15%)
  local copies, waits for them, and re-layouts  2.23 us (2%)
    all_to_all x1, blocking collectives, sum_everywhere(): piece = jnp.sum(lax.all_to_all(pieces, FAR, 0, 0, tiled=True), axis=0)  19.5 us
    all_to_all x1, blocking collectives, body(): cols = lax.all_to_all(columns, 'panel', 1, 0, tiled=True)  19.2 us
    all_to_all x1, blocking collectives, sum_everywhere(): piece = jnp.sum(lax.all_to_all(copies, NEAR, 0, 0, tiled=True), axis=0)  19.1 us
    all_to_all x1, blocking collectives, sum_everywhere(): return lax.all_to_all(copies, FAR, 0, 0, tiled=True)  18 us
    pallas_call x1, Pallas kernels, solve(): pl.pallas_call(functools.partial(solve_kernel, voxels), out_shape=jax.Sha...  11.8 us

profile of v7, /device:TPU:8, one launch (start us, length us, event | category | flops | bytes accessed | tf_op | source)
XLA Modules:
  0.0 91.7 jit_solution(14991106047837351904)
XLA Ops:
  0.0 1.3 %copy.11 = f32[8,4,8,1024]{3,2,0,1:T(8,128)S(1)} copy(f32[8,4,8,1024]{3,2,1,0:T(8,128)} %bitcast.14) | data formatting | bytes 2097152 | tf_op jit(solution)/shard_map/all_to_all | solution.py:299
  1.3 19.2 %all_to_all.34 = f32[64,4,1024]{2,0,1:T(8,128)S(1)} all-to-all(f32[64,4,1024]{2,0,1:T(8,128)S(1)} %bitcast.13), channel_id=1, replica_groups=mesh['z'=8,'y'=8,'core'=2,'panel'=4] {'panel'}, dimensions={1} | all-to-all | bytes 2097152 | tf_op jit(solution)/shard_map/all_to_all | solution.py:299
  20.5 0.0 copy-start.1
  20.5 0.7 copy-done.1
  21.2 1.6 %pack.1 = f32[32,1,2176]{2,1,0:T(1,128)S(1)} custom-call(f32[256,1024]{1,0:T(8,128)S(1)} %bitcast.9, s32[2,128]{1,0:T(2,128)S(1)} %bitcast.12), custom_call_target="tpu_custom_call" | custom-call | tf_op jit(solution)/shard_map/pack/pallas_call | solution.py:174
  22.8 19.5 %all_to_all.35 = f32[32,1,2176]{2,1,0:T(1,128)S(1)} all-to-all(f32[32,1,2176]{2,1,0:T(1,128)S(1)} %pack.1), channel_id=1, replica_groups=mesh['z'=8,'y'=8,'core'=2,'panel'=4] {'panel','y'}, dimensions={0} | all-to-all | bytes 557056 | tf_op jit(solution)/shard_map/all_to_all | solution.py:289
  42.3 0.2 reduce_sum.18
  42.5 0.1 broadcast_in_dim.4
  42.6 19.1 %all_to_all.36 = f32[16,1,2176]{2,1,0:T(1,128)S(1)} all-to-all(f32[16,1,2176]{2,1,0:T(1,128)S(1)} %broadcast_in_dim.4), channel_id=1, replica_groups=mesh['z'=8,'y'=8,'core'=2,'panel'=4] {'z','core'}, dimensions={0} | all-to-all | bytes 278528 | tf_op jit(solution)/shard_map/all_to_all | solution.py:291
  61.7 0.1 reduce_sum.19
  61.8 0.1 broadcast_in_dim.5
  61.9 0.0 copy-start
  61.9 18.0 %all_to_all.37.packed_ref = f32[32,1,2176]{2,1,0:T(1,128)S(1)} all-to-all(f32[32,1,2176]{2,1,0:T(1,128)S(1)} %broadcast_in_dim.5), channel_id=1, replica_groups=mesh['z'=8,'y'=8,'core'=2,'panel'=4] {'panel','y'}, dimensions={0} | all-to-all | bytes 557056 | tf_op jit(solution)/shard_map/all_to_all | solution.py:293
  79.9 0.0 copy-done
  79.9 11.8 %solve.1 = f32[32,1024]{1,0:T(8,128)} custom-call(f32[32,1,2176]{2,1,0:T(1,128)S(1)} %all_to_all.37.packed_ref, f32[32,256]{1,0:T(8,128)S(1)} %bitcast.11, f32[256,1024]{1,0:T(8,128)S(1)} %bitcast.10), custom_call_target="tpu_custom_call" | custom-call | tf_op jit(solution)/shard_map/solve/pallas_call | solution.py:268
Async XLA Ops:
  20.5 0.7 copy-start.1
  61.9 18.0 %copy-start = (f32[256,32]{0,1:T(8,128)S(1)}, f32[256,32]{0,1:T(8,128)}, u32[]{:S(2)}) copy-start(f32[256,32]{0,1:T(8,128)} %param.5) | copy-start | bytes 98308

commit v8 on v7

--- a/solution.py
+++ b/solution.py
@@ -17,8 +17,8 @@
 EARLY = 4
 SUBS = 1
 
-FAR = ("panel", "y")
-NEAR = ("z", "core")
+FAR = ("panel", "z")
+NEAR = ("y", "core")
 ROWS = ("z", "y", "core")
 
 
@@ -106,7 +106,7 @@
         if k + 1 < size:
             nq, nr = divmod(k + 1, SUB)
             beside = spread(cols[k, nq], nr)
-            square_rough = (beside * beside) * rough
+            square_rough = beside * (beside * rough)
             pivot = spread(cols[k + 1, nq], nr) - square_rough * (2.0 - near_one)
         lower = {q: cols[k, q] for q in range(kq, blocks)}
         lower[kq] = jnp.where(row > kr, lower[kq], 0.0)
@@ -181,7 +181,7 @@
     )(cols, pivots.reshape(-1, LANES))
 
 
-def solve_kernel(voxels, packed_ref, start_ref, cols_ref, out_ref, work, gram, basis, gram_parts, inverse_parts, cols_parts):
+def solve_kernel(voxels, packed_ref, start_ref, cols_ref, out_ref, work, gram, gram_parts, inverse_parts, cols_parts):
     size = cols_ref.shape[0]
     rank = start_ref.shape[0]
     far, subs, width = packed_ref.shape
@@ -245,21 +245,24 @@
     def by(ref, x):
         return by_parts(x, (ref[0], ref[1], ref[2]))
 
+    def factor_of(image, pushed):
+        small = dot(image, pushed, ROWS_BY_ROWS)
+        small = jnp.concatenate([small, jnp.zeros((rank, LANES - rank), jnp.float32)], axis=1)
+        return inverse_factor(small, rank)
+
     def iterate(step, carry):
         image, pushed = carry
-        small = dot(image, pushed, ROWS_BY_ROWS)
-        small = jnp.concatenate([small, jnp.zeros((rank, LANES - rank), jnp.float32)], axis=1)
-        factor = inverse_factor(small, rank)
+        factor = factor_of(image, pushed)
         top = jnp.max(jnp.max(jnp.abs(pushed), axis=0, keepdims=True), axis=1, keepdims=True)
         ahead = by(inverse_parts, pushed * (1.0 / top))
         ahead_pushed = by(gram_parts, ahead)
-        basis[...] = by_factor(factor, image)
         scaled_factor = factor * top
         return by_factor(scaled_factor, ahead), by_factor(scaled_factor, ahead_pushed)
 
     image = by(inverse_parts, by(gram_parts, start_ref[...]))
-    lax.fori_loop(0, ITERS, iterate, (image, by(gram_parts, image)))
-    out_ref[...] = by(cols_parts, basis[...])
+    image, pushed = lax.fori_loop(0, ITERS - 1, iterate, (image, by(gram_parts, image)))
+    volumes = by(cols_parts, image)
+    out_ref[...] = by_factor(factor_of(image, pushed), volumes)
 
 
 def solve(packed, start, cols, voxels):
@@ -273,7 +276,6 @@
         scratch_shapes=[
             pltpu.VMEM((size, size), jnp.float32),
             pltpu.VMEM((size, size), jnp.float32),
-            pltpu.VMEM((rank, size), jnp.float32),
             pltpu.VMEM((3, size, size), jnp.bfloat16),
             pltpu.VMEM((3, size, size), jnp.bfloat16),
             pltpu.VMEM((3, size, width), jnp.bfloat16),

time: 92.1 us -> 91.2 us (level)
  the two profiles are of different devices: /device:TPU:8 before, /device:TPU:1 now
where the time goes in v8:
time: 91.2 us; the launch traced here: 90.9 us
  blocking collectives  75 us (82%)
  Pallas kernels  13.3 us (15%)
  local copies, waits for them, and re-layouts  2.23 us (2%)
    all_to_all x1, blocking collectives, sum_everywhere(): piece = jnp.sum(lax.all_to_all(pieces, FAR, 0, 0, tiled=True), axis=0)  24.3 us
    all_to_all x1, blocking collectives, sum_everywhere(): piece = jnp.sum(lax.all_to_all(copies, NEAR, 0, 0, tiled=True), axis=0)  20.1 us
    all_to_all x1, blocking collectives, sum_everywhere(): return lax.all_to_all(copies, FAR, 0, 0, tiled=True)  15.6 us
    all_to_all x1, blocking collectives, body(): cols = lax.all_to_all(columns, 'panel', 1, 0, tiled=True)  15.1 us
    pallas_call x1, Pallas kernels, solve(): pl.pallas_call(functools.partial(solve_kernel, voxels), out_shape=jax.Sha...  11.7 us

profile of v8, /device:TPU:1, one launch (start us, length us, event | category | flops | bytes accessed | tf_op | source)
XLA Modules:
  0.0 90.9 jit_solution(11677606899347600088)
XLA Ops:
  0.0 1.3 %copy.11 = f32[8,4,8,1024]{3,2,0,1:T(8,128)S(1)} copy(f32[8,4,8,1024]{3,2,1,0:T(8,128)} %bitcast.14) | data formatting | bytes 2097152 | tf_op jit(solution)/shard_map/all_to_all | solution.py:301
  1.3 15.1 %all_to_all.34 = f32[64,4,1024]{2,0,1:T(8,128)S(1)} all-to-all(f32[64,4,1024]{2,0,1:T(8,128)S(1)} %bitcast.13), channel_id=1, replica_groups=mesh['z'=8,'y'=8,'core'=2,'panel'=4] {'panel'}, dimensions={1} | all-to-all | bytes 2097152 | tf_op jit(solution)/shard_map/all_to_all | solution.py:301
  16.4 0.0 copy-start.1
  16.4 0.7 copy-done.1
  17.1 1.6 %pack.1 = f32[32,1,2176]{2,1,0:T(1,128)S(1)} custom-call(f32[256,1024]{1,0:T(8,128)S(1)} %bitcast.9, s32[2,128]{1,0:T(2,128)S(1)} %bitcast.12), custom_call_target="tpu_custom_call" | custom-call | tf_op jit(solution)/shard_map/pack/pallas_call | solution.py:174
  18.7 24.3 %all_to_all.35 = f32[32,1,2176]{2,1,0:T(1,128)S(1)} all-to-all(f32[32,1,2176]{2,1,0:T(1,128)S(1)} %pack.1), channel_id=1, replica_groups=mesh['z'=8,'y'=8,'core'=2,'panel'=4] {'panel','z'}, dimensions={0} | all-to-all | bytes 557056 | tf_op jit(solution)/shard_map/all_to_all | solution.py:291
  43.0 0.2 reduce_sum.18
  43.2 0.1 broadcast_in_dim.4
  43.2 20.1 %all_to_all.36 = f32[16,1,2176]{2,1,0:T(1,128)S(1)} all-to-all(f32[16,1,2176]{2,1,0:T(1,128)S(1)} %broadcast_in_dim.4), channel_id=1, replica_groups=mesh['z'=8,'y'=8,'core'=2,'panel'=4] {'y','core'}, dimensions={0} | all-to-all | bytes 278528 | tf_op jit(solution)/shard_map/all_to_all | solution.py:293
  63.3 0.1 reduce_sum.19
  63.4 0.1 broadcast_in_dim.5
  63.6 0.0 copy-start
  63.6 15.6 %all_to_all.37.packed_ref = f32[32,1,2176]{2,1,0:T(1,128)S(1)} all-to-all(f32[32,1,2176]{2,1,0:T(1,128)S(1)} %broadcast_in_dim.5), channel_id=1, replica_groups=mesh['z'=8,'y'=8,'core'=2,'panel'=4] {'panel','z'}, dimensions={0} | all-to-all | bytes 557056 | tf_op jit(solution)/shard_map/all_to_all | solution.py:295
  79.2 0.0 copy-done
  79.2 11.7 %solve.1 = f32[32,1024]{1,0:T(8,128)} custom-call(f32[32,1,2176]{2,1,0:T(1,128)S(1)} %all_to_all.37.packed_ref, f32[32,256]{1,0:T(8,128)S(1)} %bitcast.11, f32[256,1024]{1,0:T(8,128)S(1)} %bitcast.10), custom_call_target="tpu_custom_call" | custom-call | tf_op jit(solution)/shard_map/solve/pallas_call | solution.py:271
Async XLA Ops:
  16.4 0.7 copy-start.1
  63.6 15.6 %copy-start = (f32[256,32]{0,1:T(8,128)S(1)}, f32[256,32]{0,1:T(8,128)}, u32[]{:S(2)}) copy-start(f32[256,32]{0,1:T(8,128)} %param.5) | copy-start | bytes 98308

commit v9 on v8

--- a/solution.py
+++ b/solution.py
@@ -18,7 +18,7 @@
 SUBS = 1
 
 FAR = ("panel", "z")
-NEAR = ("y", "core")
+NEAR = ("core", "y")
 ROWS = ("z", "y", "core")
 
 

time: 91.2 us -> 90.1 us (0.988)
  the two profiles are of different devices: /device:TPU:1 before, /device:TPU:8 now
where the time goes in v9:
time: 90.1 us; the launch traced here: 89.8 us
  blocking collectives  73.9 us (82%)
  Pallas kernels  13.3 us (15%)
  local copies, waits for them, and re-layouts  2.23 us (2%)
    all_to_all x1, blocking collectives, sum_everywhere(): piece = jnp.sum(lax.all_to_all(pieces, FAR, 0, 0, tiled=True), axis=0)  22.5 us
    all_to_all x1, blocking collectives, body(): cols = lax.all_to_all(columns, 'panel', 1, 0, tiled=True)  19.2 us
    all_to_all x1, blocking collectives, sum_everywhere(): return lax.all_to_all(copies, FAR, 0, 0, tiled=True)  16.5 us
    all_to_all x1, blocking collectives, sum_everywhere(): piece = jnp.sum(lax.all_to_all(copies, NEAR, 0, 0, tiled=True), axis=0)  15.7 us
    pallas_call x1, Pallas kernels, solve(): pl.pallas_call(functools.partial(solve_kernel, voxels), out_shape=jax.Sha...  11.7 us

profile of v9, /device:TPU:8, one launch (start us, length us, event | category | flops | bytes accessed | tf_op | source)
XLA Modules:
  0.0 89.8 jit_solution(12262535008634456440)
XLA Ops:
  0.0 1.3 %copy.11 = f32[8,4,8,1024]{3,2,0,1:T(8,128)S(1)} copy(f32[8,4,8,1024]{3,2,1,0:T(8,128)} %bitcast.14) | data formatting | bytes 2097152 | tf_op jit(solution)/shard_map/all_to_all | solution.py:301
  1.3 19.2 %all_to_all.34 = f32[64,4,1024]{2,0,1:T(8,128)S(1)} all-to-all(f32[64,4,1024]{2,0,1:T(8,128)S(1)} %bitcast.13), channel_id=1, replica_groups=mesh['z'=8,'y'=8,'core'=2,'panel'=4] {'panel'}, dimensions={1} | all-to-all | bytes 2097152 | tf_op jit(solution)/shard_map/all_to_all | solution.py:301
  20.5 0.0 copy-start.1
  20.5 0.7 copy-done.1
  21.2 1.6 %pack.1 = f32[32,1,2176]{2,1,0:T(1,128)S(1)} custom-call(f32[256,1024]{1,0:T(8,128)S(1)} %bitcast.9, s32[2,128]{1,0:T(2,128)S(1)} %bitcast.12), custom_call_target="tpu_custom_call" | custom-call | tf_op jit(solution)/shard_map/pack/pallas_call | solution.py:174
  22.8 22.5 %all_to_all.35 = f32[32,1,2176]{2,1,0:T(1,128)S(1)} all-to-all(f32[32,1,2176]{2,1,0:T(1,128)S(1)} %pack.1), channel_id=1, replica_groups=mesh['z'=8,'y'=8,'core'=2,'panel'=4] {'panel','z'}, dimensions={0} | all-to-all | bytes 557056 | tf_op jit(solution)/shard_map/all_to_all | solution.py:291
  45.3 0.2 reduce_sum.18
  45.5 0.1 broadcast_in_dim.4
  45.6 15.7 %all_to_all.36 = f32[16,1,2176]{2,1,0:T(1,128)S(1)} all-to-all(f32[16,1,2176]{2,1,0:T(1,128)S(1)} %broadcast_in_dim.4), channel_id=1, replica_groups=mesh['z'=8,'y'=8,'core'=2,'panel'=4] {'core','y'}, dimensions={0} | all-to-all | bytes 278528 | tf_op jit(solution)/shard_map/all_to_all | solution.py:293
  61.3 0.1 reduce_sum.19
  61.4 0.1 broadcast_in_dim.5
  61.6 0.0 copy-start
  61.6 16.5 %all_to_all.37.packed_ref = f32[32,1,2176]{2,1,0:T(1,128)S(1)} all-to-all(f32[32,1,2176]{2,1,0:T(1,128)S(1)} %broadcast_in_dim.5), channel_id=1, replica_groups=mesh['z'=8,'y'=8,'core'=2,'panel'=4] {'panel','z'}, dimensions={0} | all-to-all | bytes 557056 | tf_op jit(solution)/shard_map/all_to_all | solution.py:295
  78.1 0.0 copy-done
  78.1 11.7 %solve.1 = f32[32,1024]{1,0:T(8,128)} custom-call(f32[32,1,2176]{2,1,0:T(1,128)S(1)} %all_to_all.37.packed_ref, f32[32,256]{1,0:T(8,128)S(1)} %bitcast.11, f32[256,1024]{1,0:T(8,128)S(1)} %bitcast.10), custom_call_target="tpu_custom_call" | custom-call | tf_op jit(solution)/shard_map/solve/pallas_call | solution.py:271
Async XLA Ops:
  20.5 0.7 copy-start.1
  61.6 16.5 %copy-start = (f32[256,32]{0,1:T(8,128)S(1)}, f32[256,32]{0,1:T(8,128)}, u32[]{:S(2)}) copy-start(f32[256,32]{0,1:T(8,128)} %param.5) | copy-start | bytes 98308

commit v10 on v9

--- a/solution.py
+++ b/solution.py
@@ -237,9 +237,12 @@
         return scaled, corner
 
     nothing = jnp.zeros((BLOCK, size), jnp.float32)
-    scaled, _ = lax.fori_loop(0, size // BLOCK, sweep, (nothing, core[:BLOCK, :LANES]))
-    update(scaled, size - BLOCK)
-    for i, part in enumerate(split(-work[...])):
+    last = size // BLOCK - 1
+    carry = lax.fori_loop(0, last, sweep, (nothing, core[:BLOCK, :LANES]))
+    scaled, _ = sweep(jnp.int32(last), carry)
+    keep = (every_row < size - BLOCK) & (every_lane < size - BLOCK)
+    kept = jnp.where(keep, work[...], 0.0)
+    for i, part in enumerate(split(by_columns(scaled, scaled) - kept)):
         inverse_parts[i] = part
 
     def by(ref, x):
@@ -259,7 +262,8 @@
         scaled_factor = factor * top
         return by_factor(scaled_factor, ahead), by_factor(scaled_factor, ahead_pushed)
 
-    image = by(inverse_parts, by(gram_parts, start_ref[...]))
+    pushed = by(gram_parts, start_ref[...])
+    image = dot(dot(pushed, scaled, ROWS_BY_ROWS), scaled) - by_parts(pushed, split(kept))
     image, pushed = lax.fori_loop(0, ITERS - 1, iterate, (image, by(gram_parts, image)))
     volumes = by(cols_parts, image)
     out_ref[...] = by_factor(factor_of(image, pushed), volumes)

time: 90.1 us -> 90 us (level)
  no operation moved by 1% of the time
where the time goes in v10:
time: 90 us; the launch traced here: 89.7 us
  blocking collectives  73.9 us (82%)
  Pallas kernels  13.2 us (15%)
  local copies, waits for them, and re-layouts  2.23 us (2%)
    all_to_all x1, blocking collectives, sum_everywhere(): piece = jnp.sum(lax.all_to_all(pieces, FAR, 0, 0, tiled=True), axis=0)  22.5 us
    all_to_all x1, blocking collectives, body(): cols = lax.all_to_all(columns, 'panel', 1, 0, tiled=True)  19.2 us
    all_to_all x1, blocking collectives, sum_everywhere(): return lax.all_to_all(copies, FAR, 0, 0, tiled=True)  16.5 us
    all_to_all x1, blocking collectives, sum_everywhere(): piece = jnp.sum(lax.all_to_all(copies, NEAR, 0, 0, tiled=True), axis=0)  15.7 us
    pallas_call x1, Pallas kernels, solve(): pl.pallas_call(functools.partial(solve_kernel, voxels), out_shape=jax.Sha...  11.6 us

profile of v10, /device:TPU:8, one launch (start us, length us, event | category | flops | bytes accessed | tf_op | source)
XLA Modules:
  0.0 89.7 jit_solution(10731749083999552718)
XLA Ops:
  0.0 1.3 %copy.11 = f32[8,4,8,1024]{3,2,0,1:T(8,128)S(1)} copy(f32[8,4,8,1024]{3,2,1,0:T(8,128)} %bitcast.14) | data formatting | bytes 2097152 | tf_op jit(solution)/shard_map/all_to_all | solution.py:305
  1.3 19.2 %all_to_all.34 = f32[64,4,1024]{2,0,1:T(8,128)S(1)} all-to-all(f32[64,4,1024]{2,0,1:T(8,128)S(1)} %bitcast.13), channel_id=1, replica_groups=mesh['z'=8,'y'=8,'core'=2,'panel'=4] {'panel'}, dimensions={1} | all-to-all | bytes 2097152 | tf_op jit(solution)/shard_map/all_to_all | solution.py:305
  20.5 0.0 copy-start.1
  20.5 0.7 copy-done.1
  21.2 1.6 %pack.1 = f32[32,1,2176]{2,1,0:T(1,128)S(1)} custom-call(f32[256,1024]{1,0:T(8,128)S(1)} %bitcast.9, s32[2,128]{1,0:T(2,128)S(1)} %bitcast.12), custom_call_target="tpu_custom_call" | custom-call | tf_op jit(solution)/shard_map/pack/pallas_call | solution.py:174
  22.8 22.5 %all_to_all.35 = f32[32,1,2176]{2,1,0:T(1,128)S(1)} all-to-all(f32[32,1,2176]{2,1,0:T(1,128)S(1)} %pack.1), channel_id=1, replica_groups=mesh['z'=8,'y'=8,'core'=2,'panel'=4] {'panel','z'}, dimensions={0} | all-to-all | bytes 557056 | tf_op jit(solution)/shard_map/all_to_all | solution.py:295
  45.3 0.2 reduce_sum.18
  45.5 0.1 broadcast_in_dim.4
  45.6 15.7 %all_to_all.36 = f32[16,1,2176]{2,1,0:T(1,128)S(1)} all-to-all(f32[16,1,2176]{2,1,0:T(1,128)S(1)} %broadcast_in_dim.4), channel_id=1, replica_groups=mesh['z'=8,'y'=8,'core'=2,'panel'=4] {'core','y'}, dimensions={0} | all-to-all | bytes 278528 | tf_op jit(solution)/shard_map/all_to_all | solution.py:297
  61.3 0.1 reduce_sum.19
  61.4 0.1 broadcast_in_dim.5
  61.6 0.0 copy-start
  61.6 16.5 %all_to_all.37.packed_ref = f32[32,1,2176]{2,1,0:T(1,128)S(1)} all-to-all(f32[32,1,2176]{2,1,0:T(1,128)S(1)} %broadcast_in_dim.5), channel_id=1, replica_groups=mesh['z'=8,'y'=8,'core'=2,'panel'=4] {'panel','z'}, dimensions={0} | all-to-all | bytes 557056 | tf_op jit(solution)/shard_map/all_to_all | solution.py:299
  78.1 0.0 copy-done
  78.1 11.6 %solve.1 = f32[32,1024]{1,0:T(8,128)} custom-call(f32[32,1,2176]{2,1,0:T(1,128)S(1)} %all_to_all.37.packed_ref, f32[32,256]{1,0:T(8,128)S(1)} %bitcast.11, f32[256,1024]{1,0:T(8,128)S(1)} %bitcast.10), custom_call_target="tpu_custom_call" | custom-call | tf_op jit(solution)/shard_map/solve/pallas_call | solution.py:275
Async XLA Ops:
  20.5 0.7 copy-start.1
  61.6 16.5 %copy-start = (f32[256,32]{0,1:T(8,128)S(1)}, f32[256,32]{0,1:T(8,128)}, u32[]{:S(2)}) copy-start(f32[256,32]{0,1:T(8,128)} %param.5) | copy-start | bytes 98308

commit v11 on v10

--- a/solution.py
+++ b/solution.py
@@ -17,8 +17,8 @@
 EARLY = 4
 SUBS = 1
 
-FAR = ("panel", "z")
-NEAR = ("core", "y")
+FAR = ("panel", "y")
+NEAR = ("core", "z")
 ROWS = ("z", "y", "core")
 
 

time: 90 us -> 89.9 us (level)
    all_to_all x1, blocking collectives: 22.5 us -> 19.5 us  [sum_everywhere(): piece = jnp.sum(lax.all_to_all(pieces, FAR, 0, 0, tiled=True), axis=0)]
    all_to_all x1, blocking collectives: 15.7 us -> 18.7 us  [sum_everywhere(): piece = jnp.sum(lax.all_to_all(copies, NEAR, 0, 0, tiled=True), axis=0)]
where the time goes in v11:
time: 89.9 us; the launch traced here: 89.6 us
  blocking collectives  73.9 us (82%)
  Pallas kernels  13.2 us (15%)
  local copies, waits for them, and re-layouts  2.23 us (2%)
    all_to_all x1, blocking collectives, sum_everywhere(): piece = jnp.sum(lax.all_to_all(pieces, FAR, 0, 0, tiled=True), axis=0)  19.5 us
    all_to_all x1, blocking collectives, body(): cols = lax.all_to_all(columns, 'panel', 1, 0, tiled=True)  19.2 us
    all_to_all x1, blocking collectives, sum_everywhere(): piece = jnp.sum(lax.all_to_all(copies, NEAR, 0, 0, tiled=True), axis=0)  18.7 us
    all_to_all x1, blocking collectives, sum_everywhere(): return lax.all_to_all(copies, FAR, 0, 0, tiled=True)  16.5 us
    pallas_call x1, Pallas kernels, solve(): pl.pallas_call(functools.partial(solve_kernel, voxels), out_shape=jax.Sha...  11.6 us

profile of v11, /device:TPU:8, one launch (start us, length us, event | category | flops | bytes accessed | tf_op | source)
XLA Modules:
  0.0 89.6 jit_solution(2080275639944067150)
XLA Ops:
  0.0 1.3 %copy.11 = f32[8,4,8,1024]{3,2,0,1:T(8,128)S(1)} copy(f32[8,4,8,1024]{3,2,1,0:T(8,128)} %bitcast.14) | data formatting | bytes 2097152 | tf_op jit(solution)/shard_map/all_to_all | solution.py:305
  1.3 19.2 %all_to_all.34 = f32[64,4,1024]{2,0,1:T(8,128)S(1)} all-to-all(f32[64,4,1024]{2,0,1:T(8,128)S(1)} %bitcast.13), channel_id=1, replica_groups=mesh['z'=8,'y'=8,'core'=2,'panel'=4] {'panel'}, dimensions={1} | all-to-all | bytes 2097152 | tf_op jit(solution)/shard_map/all_to_all | solution.py:305
  20.5 0.0 copy-start.1
  20.5 0.7 copy-done.1
  21.2 1.6 %pack.1 = f32[32,1,2176]{2,1,0:T(1,128)S(1)} custom-call(f32[256,1024]{1,0:T(8,128)S(1)} %bitcast.9, s32[2,128]{1,0:T(2,128)S(1)} %bitcast.12), custom_call_target="tpu_custom_call" | custom-call | tf_op jit(solution)/shard_map/pack/pallas_call | solution.py:174
  22.8 19.5 %all_to_all.35 = f32[32,1,2176]{2,1,0:T(1,128)S(1)} all-to-all(f32[32,1,2176]{2,1,0:T(1,128)S(1)} %pack.1), channel_id=1, replica_groups=mesh['z'=8,'y'=8,'core'=2,'panel'=4] {'panel','y'}, dimensions={0} | all-to-all | bytes 557056 | tf_op jit(solution)/shard_map/all_to_all | solution.py:295
  42.3 0.2 reduce_sum.18
  42.5 0.1 broadcast_in_dim.4
  42.6 18.7 %all_to_all.36 = f32[16,1,2176]{2,1,0:T(1,128)S(1)} all-to-all(f32[16,1,2176]{2,1,0:T(1,128)S(1)} %broadcast_in_dim.4), channel_id=1, replica_groups=mesh['z'=8,'y'=8,'core'=2,'panel'=4] {'core','z'}, dimensions={0} | all-to-all | bytes 278528 | tf_op jit(solution)/shard_map/all_to_all | solution.py:297
  61.3 0.1 reduce_sum.19
  61.4 0.1 broadcast_in_dim.5
  61.5 0.0 copy-start
  61.5 16.5 %all_to_all.37.packed_ref = f32[32,1,2176]{2,1,0:T(1,128)S(1)} all-to-all(f32[32,1,2176]{2,1,0:T(1,128)S(1)} %broadcast_in_dim.5), channel_id=1, replica_groups=mesh['z'=8,'y'=8,'core'=2,'panel'=4] {'panel','y'}, dimensions={0} | all-to-all | bytes 557056 | tf_op jit(solution)/shard_map/all_to_all | solution.py:299
  78.0 0.0 copy-done
  78.0 11.6 %solve.1 = f32[32,1024]{1,0:T(8,128)} custom-call(f32[32,1,2176]{2,1,0:T(1,128)S(1)} %all_to_all.37.packed_ref, f32[32,256]{1,0:T(8,128)S(1)} %bitcast.11, f32[256,1024]{1,0:T(8,128)S(1)} %bitcast.10), custom_call_target="tpu_custom_call" | custom-call | tf_op jit(solution)/shard_map/solve/pallas_call | solution.py:275
Async XLA Ops:
  20.5 0.7 copy-start.1
  61.5 16.5 %copy-start = (f32[256,32]{0,1:T(8,128)S(1)}, f32[256,32]{0,1:T(8,128)}, u32[]{:S(2)}) copy-start(f32[256,32]{0,1:T(8,128)} %param.5) | copy-start | bytes 98308

commit v12 on v10

--- a/solution.py
+++ b/solution.py
@@ -181,7 +181,7 @@
     )(cols, pivots.reshape(-1, LANES))
 
 
-def solve_kernel(voxels, packed_ref, start_ref, cols_ref, out_ref, work, gram, gram_parts, inverse_parts, cols_parts):
+def solve_kernel(voxels, packed_ref, start_ref, cols_ref, out_ref, work, square, gram_parts, inverse_parts, cols_parts):
     size = cols_ref.shape[0]
     rank = start_ref.shape[0]
     far, subs, width = packed_ref.shape
@@ -196,7 +196,8 @@
             diagonal.append(tail[:, h : h + 1])
     packed = jnp.concatenate(rows, axis=0)
     flipped = packed.T
-    gram[...] = jnp.where(every_row >= every_lane, packed, flipped) * (1.0 / voxels)
+    square[0] = packed
+    square[1] = flipped
     core = jnp.where(every_row < every_lane, packed, flipped)
     core = jnp.where(every_row == every_lane, jnp.concatenate(diagonal, axis=0), core) * (1.0 / size)
     core = core + jnp.where(every_row == every_lane, CORE_SHIFT, 0.0)
@@ -232,7 +233,9 @@
         scaled = by_factor(factor, band)
         for i, part in enumerate(split(cols_ref[rows_here, :])):
             cols_parts[i, rows_here, :] = part
-        for i, part in enumerate(split(gram[rows_here, :])):
+        below = row + base >= lane
+        gram = jnp.where(below, square[0, rows_here, :], square[1, rows_here, :]) * (1.0 / voxels)
+        for i, part in enumerate(split(gram)):
             gram_parts[i, rows_here, :] = part
         return scaled, corner
 
@@ -279,7 +282,7 @@
         out_specs=pl.BlockSpec(memory_space=pltpu.VMEM),
         scratch_shapes=[
             pltpu.VMEM((size, size), jnp.float32),
-            pltpu.VMEM((size, size), jnp.float32),
+            pltpu.VMEM((2, size, size), jnp.float32),
             pltpu.VMEM((3, size, size), jnp.bfloat16),
             pltpu.VMEM((3, size, size), jnp.bfloat16),
             pltpu.VMEM((3, size, width), jnp.bfloat16),

time: 90 us -> 90 us (level)
  no operation moved by 1% of the time
where the time goes in v12:
time: 90 us; the launch traced here: 89.7 us
  blocking collectives  73.9 us (82%)
  Pallas kernels  13.2 us (15%)
  local copies, waits for them, and re-layouts  2.23 us (2%)
    all_to_all x1, blocking collectives, sum_everywhere(): piece = jnp.sum(lax.all_to_all(pieces, FAR, 0, 0, tiled=True), axis=0)  22.5 us
    all_to_all x1, blocking collectives, body(): cols = lax.all_to_all(columns, 'panel', 1, 0, tiled=True)  19.2 us
    all_to_all x1, blocking collectives, sum_everywhere(): return lax.all_to_all(copies, FAR, 0, 0, tiled=True)  16.5 us
    all_to_all x1, blocking collectives, sum_everywhere(): piece = jnp.sum(lax.all_to_all(copies, NEAR, 0, 0, tiled=True), axis=0)  15.7 us
    pallas_call x1, Pallas kernels, solve(): pl.pallas_call(functools.partial(solve_kernel, voxels), out_shape=jax.Sha...  11.6 us

profile of v12, /device:TPU:8, one launch (start us, length us, event | category | flops | bytes accessed | tf_op | source)
XLA Modules:
  0.0 89.7 jit_solution(4050766795952717890)
XLA Ops:
  0.0 1.3 %copy.11 = f32[8,4,8,1024]{3,2,0,1:T(8,128)S(1)} copy(f32[8,4,8,1024]{3,2,1,0:T(8,128)} %bitcast.14) | data formatting | bytes 2097152 | tf_op jit(solution)/shard_map/all_to_all | solution.py:308
  1.3 19.2 %all_to_all.34 = f32[64,4,1024]{2,0,1:T(8,128)S(1)} all-to-all(f32[64,4,1024]{2,0,1:T(8,128)S(1)} %bitcast.13), channel_id=1, replica_groups=mesh['z'=8,'y'=8,'core'=2,'panel'=4] {'panel'}, dimensions={1} | all-to-all | bytes 2097152 | tf_op jit(solution)/shard_map/all_to_all | solution.py:308
  20.5 0.0 copy-start.1
  20.5 0.7 copy-done.1
  21.2 1.6 %pack.1 = f32[32,1,2176]{2,1,0:T(1,128)S(1)} custom-call(f32[256,1024]{1,0:T(8,128)S(1)} %bitcast.9, s32[2,128]{1,0:T(2,128)S(1)} %bitcast.12), custom_call_target="tpu_custom_call" | custom-call | tf_op jit(solution)/shard_map/pack/pallas_call | solution.py:174
  22.8 22.5 %all_to_all.35 = f32[32,1,2176]{2,1,0:T(1,128)S(1)} all-to-all(f32[32,1,2176]{2,1,0:T(1,128)S(1)} %pack.1), channel_id=1, replica_groups=mesh['z'=8,'y'=8,'core'=2,'panel'=4] {'panel','z'}, dimensions={0} | all-to-all | bytes 557056 | tf_op jit(solution)/shard_map/all_to_all | solution.py:298
  45.3 0.2 reduce_sum.18
  45.5 0.1 broadcast_in_dim.4
  45.6 15.7 %all_to_all.36 = f32[16,1,2176]{2,1,0:T(1,128)S(1)} all-to-all(f32[16,1,2176]{2,1,0:T(1,128)S(1)} %broadcast_in_dim.4), channel_id=1, replica_groups=mesh['z'=8,'y'=8,'core'=2,'panel'=4] {'core','y'}, dimensions={0} | all-to-all | bytes 278528 | tf_op jit(solution)/shard_map/all_to_all | solution.py:300
  61.3 0.1 reduce_sum.19
  61.4 0.1 broadcast_in_dim.5
  61.6 0.0 copy-start
  61.6 16.5 %all_to_all.37.packed_ref = f32[32,1,2176]{2,1,0:T(1,128)S(1)} all-to-all(f32[32,1,2176]{2,1,0:T(1,128)S(1)} %broadcast_in_dim.5), channel_id=1, replica_groups=mesh['z'=8,'y'=8,'core'=2,'panel'=4] {'panel','z'}, dimensions={0} | all-to-all | bytes 557056 | tf_op jit(solution)/shard_map/all_to_all | solution.py:302
  78.1 0.0 copy-done
  78.1 11.6 %solve.1 = f32[32,1024]{1,0:T(8,128)} custom-call(f32[32,1,2176]{2,1,0:T(1,128)S(1)} %all_to_all.37.packed_ref, f32[32,256]{1,0:T(8,128)S(1)} %bitcast.11, f32[256,1024]{1,0:T(8,128)S(1)} %bitcast.10), custom_call_target="tpu_custom_call" | custom-call | tf_op jit(solution)/shard_map/solve/pallas_call | solution.py:278
Async XLA Ops:
  20.5 0.7 copy-start.1
  61.6 16.5 %copy-start = (f32[256,32]{0,1:T(8,128)S(1)}, f32[256,32]{0,1:T(8,128)}, u32[]{:S(2)}) copy-start(f32[256,32]{0,1:T(8,128)} %param.5) | copy-start | bytes 98308
